TPU v7x, 32 devices: a whole 2x2x4 slice. The times are simulated.
32 devices in a mesh: state: 2 (over x), mode: 16 (over z, y, core).
Axes of the slice: x: 2, y: 2, z: 4, core: 2. Of those that a mesh axis runs over, the one named last changes fastest.
Arguments:
- core: bfloat16 [2, 512, 512, 256], P('state', 'mode'), may hold values from -6 to 6
- op_one: bfloat16 [2, 3, 512, 512], replicated, may hold values from -0.25 to 0.25
- op_two: bfloat16 [2, 3, 512, 512], replicated, may hold values from -0.25 to 0.25
- op_three: bfloat16 [2, 3, 256, 256], replicated, may hold values from -0.375 to 0.375
Outputs:
- relaxed: float32 [2, 512, 512, 256], P('state', 'mode')
All inputs are finite; a program needn't handle non-finite values.
Results may differ from a plain program's by a relative error of at most 0.0033.
Values may be sent and summed in bfloat16 or wider, within the bound.
A program may use at most 192 MiB of HBM per device.

v0:
```python
import jax
import jax.numpy as jnp
from jax import lax
from jax.sharding import PartitionSpec as P


def swapped(block, axis, distance):
    count = lax.axis_size(axis)
    route = []
    for low in range(count):
        high = low | 1 << distance
        if high != low and high < count:
            route += [(low, high), (high, low)]
    return lax.ppermute(block, axis, route)


def mode_two_three(block, second, third):
    inner = jnp.einsum("ijk,lk->ijl", block, third, preferred_element_type=jnp.float32).astype(
        jnp.bfloat16
    )
    return jnp.einsum("ab,ibk->iak", second, inner, preferred_element_type=jnp.float32).astype(
        jnp.bfloat16
    )


def shards(core, op_one, op_two, op_three):
    own_core = core[0]
    term_count = op_one.shape[1]
    state_index = lax.axis_index("state")
    own_first = lax.dynamic_index_in_dim(op_one, state_index, 0, keepdims=False)
    own_second = lax.dynamic_index_in_dim(op_two, state_index, 0, keepdims=False)
    own_third = lax.dynamic_index_in_dim(op_three, state_index, 0, keepdims=False)
    sources = [own_core for term in range(term_count)]
    firsts = [own_first[term] for term in range(term_count)]
    seconds = [own_second[term] for term in range(term_count)]
    thirds = [own_third[term] for term in range(term_count)]
    prepared = [
        mode_two_three(sources[term], seconds[term], thirds[term]) for term in range(term_count)
    ]
    results = []
    for term in range(term_count):
        matrix = firsts[term]

        def mode_one_term(piece, matrix=matrix):
            return jnp.einsum("ab,bjk->ajk", matrix, piece, preferred_element_type=jnp.float32)

        results.append(
            mode_one_term(
                lax.all_to_all(prepared[term], "mode", split_axis=1, concat_axis=0, tiled=True)
            )
        )
    diagonal = results[0] + results[1]
    coupled = results[2]
    combined = diagonal + swapped(coupled, "state", 0)
    applied = combined.astype(jnp.bfloat16)
    returned = lax.all_to_all(applied, "mode", split_axis=0, concat_axis=1, tiled=True)
    relaxed = own_core.astype(jnp.float32) - 0.5 * returned.astype(jnp.float32)
    return relaxed[None]


def solution(mesh):
    placed = (P("state", "mode", None, None), P(), P(), P())
    return jax.shard_map(
        shards,
        mesh=mesh,
        in_specs=placed,
        out_specs=P("state", "mode", None, None),
        check_vma=False,
    )
```

profile of v0, /device:TPU:24, one launch (start us, length us, event | category | flops | bytes accessed | tf_op | source)
XLA Modules:
  0.0 1028.9 jit_solution(6362954320374835543)
XLA Ops:
  0.0 0.0 copy-start
  0.0 1.9 copy-done
  1.9 11.2 %convert_bitcast_fusion = bf16[32,512,256]{1,2,0:T(8,128)(2,1)} fusion(bf16[1,32,512,256]{3,2,1,0:T(8,128)(2,1)} %param.4, bf16[2,3,512,512]{3,2,1,0:T(8,128)(2,1)S(1)} %copy-done, s32[]{:T(128)S(6)} %select_n.7, s32[]{:T(128)S(6)} %add.19, bf16[2,3,256,256]{3,2,1,0:T(8,128)(2,1)} %param.7), kind=kOutput, calls=%fused_computation.15 | convolution fusion | flops 6450839552 | bytes 17434624 | tf_op jit(solution)/shard_map/ab,ibk->iak/dot_general | solution.py:21
  13.1 14.6 %copy.22 = bf16[32,512,256]{2,0,1:T(8,128)(2,1)} copy(bf16[32,512,256]{1,2,0:T(8,128)(2,1)} %convert_bitcast_fusion) | data formatting | bytes 16777216 | tf_op jit(solution)/shard_map/convert_element_type | solution.py:21
  27.6 6.1 all-to-all-start.2
  33.7 11.2 %convert_bitcast_fusion.2 = bf16[32,512,256]{1,2,0:T(8,128)(2,1)} fusion(bf16[1,32,512,256]{3,2,1,0:T(8,128)(2,1)} %param.4, bf16[2,3,512,512]{3,2,1,0:T(8,128)(2,1)S(1)} %copy-done, s32[]{:T(128)S(6)} %select_n.7, bf16[2,3,256,256]{3,2,1,0:T(8,128)(2,1)} %param.7), kind=kOutput, calls=%fused_computation.19 | convolution fusion | flops 6450839552 | bytes 17433600 | tf_op jit(solution)/shard_map/ab,ibk->iak/dot_general | solution.py:21
  44.9 14.6 %copy.16 = bf16[32,512,256]{2,0,1:T(8,128)(2,1)} copy(bf16[32,512,256]{1,2,0:T(8,128)(2,1)} %convert_bitcast_fusion.2) | data formatting | bytes 16777216 | tf_op jit(solution)/shard_map/convert_element_type | solution.py:21
  59.5 144.2 %all-to-all-done.2 = bf16[32,512,256]{2,0,1:T(8,128)(2,1)} async-done(((bf16[32,512,256]{2,0,1:T(8,128)(2,1)}), bf16[32,512,256]{2,0,1:T(8,128)(2,1)}, u32[]{:S(2)}, u32[]{:S(2)}) %all-to-all-start.2) | async-done | bytes 8388640 | tf_op jit(solution)/shard_map/all_to_all | solution.py:49
  203.7 17.3 %all-to-all-start = ((bf16[32,512,256]{2,0,1:T(8,128)(2,1)}), bf16[32,512,256]{2,0,1:T(8,128)(2,1)}, u32[]{:S(2)}, u32[]{:S(2)}) async-start(bf16[32,512,256]{2,0,1:T(8,128)(2,1)} %copy.16), calls=%async_computation | async-start | bytes 16777216 | tf_op jit(solution)/shard_map/all_to_all | solution.py:49
  221.0 11.2 %convert_bitcast_fusion.1 = bf16[32,512,256]{1,2,0:T(8,128)(2,1)} fusion(bf16[1,32,512,256]{3,2,1,0:T(8,128)(2,1)} %param.4, bf16[2,3,512,512]{3,2,1,0:T(8,128)(2,1)S(1)} %copy-done, s32[]{:T(128)S(6)} %select_n.7, s32[]{:T(128)S(6)} %add.16, bf16[2,3,256,256]{3,2,1,0:T(8,128)(2,1)} %param.7), kind=kOutput, calls=%fused_computation.17 | convolution fusion | flops 6450839552 | bytes 17434624 | tf_op jit(solution)/shard_map/ab,ibk->iak/dot_general | solution.py:21
  232.2 14.6 %copy.19 = bf16[32,512,256]{2,0,1:T(8,128)(2,1)} copy(bf16[32,512,256]{1,2,0:T(8,128)(2,1)} %convert_bitcast_fusion.1) | data formatting | bytes 16777216 | tf_op jit(solution)/shard_map/convert_element_type | solution.py:21
  246.8 8.0 copy.24
  254.8 0.0 copy-start.2
  254.8 136.2 %all-to-all-done = bf16[32,512,256]{2,0,1:T(8,128)(2,1)} async-done(((bf16[32,512,256]{2,0,1:T(8,128)(2,1)}), bf16[32,512,256]{2,0,1:T(8,128)(2,1)}, u32[]{:S(2)}, u32[]{:S(2)}) %all-to-all-start) | async-done | bytes 8388640 | tf_op jit(solution)/shard_map/all_to_all | solution.py:49
  391.0 17.3 %all-to-all-start.1 = ((bf16[32,512,256]{2,0,1:T(8,128)(2,1)}), bf16[32,512,256]{2,0,1:T(8,128)(2,1)}, u32[]{:S(2)}, u32[]{:S(2)}) async-start(bf16[32,512,256]{2,0,1:T(8,128)(2,1)} %copy.19), calls=%async_computation.1 | async-start | bytes 16777216 | tf_op jit(solution)/shard_map/all_to_all | solution.py:49
  408.2 0.0 copy-done.2
  408.2 11.9 %fusion.33 = f32[512,32,256]{2,0,1:T(8,128)} fusion(bf16[512,32,256]{2,0,1:T(8,128)(2,1)} %bitcast.110, bf16[2,3,512,512]{3,2,1,0:T(8,128)(2,1)S(1)} %copy-done.2, s32[]{:T(128)S(6)} %select_n.7, s32[]{:T(128)S(6)} %add.19), kind=kOutput, calls=%fused_computation.23 | convolution fusion | flops 4294967296 | bytes 25690120 | tf_op jit(solution)/shard_map/ab,bjk->ajk/dot_general | solution.py:45
  420.1 1.5 collective-permute-start
  421.6 8.0 copy.18
  429.7 148.6 %all-to-all-done.1 = bf16[32,512,256]{2,0,1:T(8,128)(2,1)} async-done(((bf16[32,512,256]{2,0,1:T(8,128)(2,1)}), bf16[32,512,256]{2,0,1:T(8,128)(2,1)}, u32[]{:S(2)}, u32[]{:S(2)}) %all-to-all-start.1) | async-done | bytes 8388640 | tf_op jit(solution)/shard_map/all_to_all | solution.py:49
  578.2 8.0 copy.21
  586.3 11.5 %fusion.34 = f32[512,32,256]{2,0,1:T(8,128)} fusion(bf16[512,32,256]{2,0,1:T(8,128)(2,1)} %bitcast.111, bf16[2,3,512,512]{3,2,1,0:T(8,128)(2,1)S(1)} %copy-done.2, s32[]{:T(128)S(6)} %select_n.7), kind=kOutput, calls=%fused_computation.28 | convolution fusion | flops 4294967296 | bytes 25690116 | tf_op jit(solution)/shard_map/ab,bjk->ajk/dot_general | solution.py:45
  597.8 185.0 %collective-permute-done = f32[512,32,256]{2,0,1:T(8,128)} collective-permute-done((f32[512,32,256]{2,0,1:T(8,128)}, f32[512,32,256]{2,0,1:T(8,128)}, u32[]{:S(2)}, u32[]{:S(2)}) %collective-permute-start) | collective-permute-done | bytes 16777248 | tf_op jit(solution)/shard_map/ppermute | solution.py:14
  782.7 18.8 %add_convert_fusion = bf16[512,32,256]{2,0,1:T(8,128)(2,1)} fusion(f32[512,32,256]{2,0,1:T(8,128)} %collective-permute-done, f32[512,32,256]{2,0,1:T(8,128)} %fusion.34, bf16[512,32,256]{2,0,1:T(8,128)(2,1)} %bitcast.109, bf16[2,3,512,512]{3,2,1,0:T(8,128)(2,1)S(1)} %copy-done.2, s32[]{:T(128)S(6)} %select_n.7, s32[]{:T(128)S(6)} %add.16), kind=kOutput, calls=%fused_computation.1 | convolution fusion | flops 4307550208 | bytes 50855944 | tf_op jit(solution)/shard_map/ab,bjk->ajk/dot_general | solution.py:45
  801.6 11.4 %copy.25 = bf16[512,32,256]{2,1,0:T(8,128)(2,1)} copy(bf16[512,32,256]{2,0,1:T(8,128)(2,1)} %add_convert_fusion) | data formatting | bytes 16777216 | tf_op jit(solution)/shard_map/convert_element_type | solution.py:55
  813.0 187.2 %all_to_all.63 = bf16[512,32,256]{2,1,0:T(8,128)(2,1)} all-to-all(bf16[512,32,256]{2,1,0:T(8,128)(2,1)} %copy.25), channel_id=1, replica_groups=mesh['state'=2,'mode'=16] {'mode'}, dimensions={0} | all-to-all | bytes 16777216 | tf_op jit(solution)/shard_map/all_to_all | solution.py:56
  1000.2 12.0 %convert_multiply_fusion = f32[512,32,256]{2,1,0:T(8,128)} fusion(bf16[512,32,256]{2,1,0:T(8,128)(2,1)} %all_to_all.63), kind=kLoop, calls=%fused_computation | loop fusion | flops 8388608 | bytes 25165824 | tf_op jit(solution)/shard_map/mul | solution.py:57
  1012.2 6.6 copy.26
  1018.7 0.0 copy-start.1
  1018.8 10.2 convert_subtract_fusion
  1028.9 0.0 copy-done.1
Async XLA Ops:
  0.0 1.9 copy-start
  27.6 176.1 %all-to-all-start.2 = ((bf16[32,512,256]{2,0,1:T(8,128)(2,1)}), bf16[32,512,256]{2,0,1:T(8,128)(2,1)}, u32[]{:S(2)}, u32[]{:S(2)}) async-start(bf16[32,512,256]{2,0,1:T(8,128)(2,1)} %copy.22), calls=%async_computation.2 | async-start | bytes 16777216 | tf_op jit(solution)/shard_map/all_to_all | solution.py:49
  203.7 187.3 %all-to-all-start = ((bf16[32,512,256]{2,0,1:T(8,128)(2,1)}), bf16[32,512,256]{2,0,1:T(8,128)(2,1)}, u32[]{:S(2)}, u32[]{:S(2)}) async-start(bf16[32,512,256]{2,0,1:T(8,128)(2,1)} %copy.16), calls=%async_computation | async-start | bytes 16777216 | tf_op jit(solution)/shard_map/all_to_all | solution.py:49
  254.8 153.4 %copy-start.2 = (bf16[2,3,512,512]{3,2,1,0:T(8,128)(2,1)S(1)}, bf16[2,3,512,512]{3,2,1,0:T(8,128)(2,1)}, u32[]{:S(2)}) copy-start(bf16[2,3,512,512]{3,2,1,0:T(8,128)(2,1)} %param.5) | copy-start | bytes 9437188
  391.0 187.3 %all-to-all-start.1 = ((bf16[32,512,256]{2,0,1:T(8,128)(2,1)}), bf16[32,512,256]{2,0,1:T(8,128)(2,1)}, u32[]{:S(2)}, u32[]{:S(2)}) async-start(bf16[32,512,256]{2,0,1:T(8,128)(2,1)} %copy.19), calls=%async_computation.1 | async-start | bytes 16777216 | tf_op jit(solution)/shard_map/all_to_all | solution.py:49
  420.1 362.6 %collective-permute-start = (f32[512,32,256]{2,0,1:T(8,128)}, f32[512,32,256]{2,0,1:T(8,128)}, u32[]{:S(2)}, u32[]{:S(2)}) collective-permute-start(f32[512,32,256]{2,0,1:T(8,128)} %fusion.33), channel_id=1, source_target_pairs={{0,16},{16,0},{1,17},{17,1},{2,18},{18,2},{3,19},{19,3},{4,20},{20... | collective-permute-start | bytes 50331656 | tf_op jit(solution)/shard_map/ppermute | solution.py:14
  1018.7 10.2 copy-start.1
where the time goes:
time: 1030 us
  waiting for transfers between devices  614 us (60%)
  blocking collectives  187 us (18%)
  local copies, waits for them, and re-layouts  87.8 us (9%)
  matrix products  75.8 us (7%)
  starting transfers between devices  42.1 us (4%)
  other arithmetic  22.2 us (2%)
    all_to_all x3, waiting for transfers between devices, shards(): lax.all_to_all(prepared[term], 'mode', split_axis=1, concat_axis=0, tiled...  429 us
    all_to_all x1, blocking collectives, shards(): lax.all_to_all(applied, 'mode', split_axis=0, concat_axis=1, tiled=True)  187 us
    ppermute x1, waiting for transfers between devices, swapped(): return lax.ppermute(block, axis, route)  185 us
    convert_element_type x3, local copies, waits for them, and re-layouts, mode_two_three(): jnp.einsum('ab,ibk->iak', second, inner, preferred_element_type=jnp.float32)  43.8 us
    dot_general x3, matrix products, mode_one_term(): jnp.einsum('ab,bjk->ajk', matrix, piece, preferred_element_type=jnp.float32)  42.2 us
    all_to_all x3, starting transfers between devices, shards(): lax.all_to_all(prepared[term], 'mode', split_axis=1, concat_axis=0, tiled...  40.6 us
    dot_general x3, matrix products, mode_two_three(): jnp.einsum('ab,ibk->iak', second, inner, preferred_element_type=jnp.float32)  33.5 us
    all_to_all x3, local copies, waits for them, and re-layouts, shards(): lax.all_to_all(prepared[term], 'mode', split_axis=1, concat_axis=0, tiled...  24.1 us
  transfers between devices with their start and end apart: 4, of which 4 were waited for; matrix products, arithmetic and copies ran while one was open for 10% of the time, Pallas kernels for 0%

commit v1 on v0

v1 whole, which is shorter than its diff:
```python
import functools

import jax
import jax.numpy as jnp
from jax import lax
from jax.experimental import pallas as pl
from jax.experimental.pallas import tpu as pltpu
from jax.sharding import PartitionSpec as P

CHUNK_ROWS = 32
MIB = 1 << 20


def one_two_kernel(outer, terms, step_rows, *refs):
    own_ref = refs[0]
    ups = refs[1 : outer]
    downs = refs[outer : 2 * outer - 1]
    first_ref, third_ref, out_ref = refs[2 * outer - 1 :]
    place = lax.axis_index("mode") // (lax.axis_size("mode") // outer)

    def body(row, carry):
        blocks = [own_ref[row]]
        for hop in range(1, outer):
            blocks.append(
                jnp.where(place >= hop, ups[hop - 1][row], downs[outer - hop - 1][row])
            )
        block = jnp.concatenate(blocks, axis=0) if len(blocks) > 1 else blocks[0]
        for term in range(terms):
            inner = jnp.dot(block, third_ref[term], preferred_element_type=jnp.float32)
            value = jnp.dot(
                first_ref[term], inner.astype(jnp.bfloat16), preferred_element_type=jnp.float32
            )
            out_ref[term, row] = value.astype(jnp.bfloat16)
        return carry

    lax.fori_loop(0, step_rows, body, 0)


def one_three(own, ups, downs, first, third):
    rows, held, depth = own.shape
    terms, made, _ = first.shape
    outer = len(ups) + 1
    step_rows = min(rows, 8)
    piece = pl.BlockSpec((step_rows, held, depth), lambda i: (i, 0, 0))
    whole = lambda shape: pl.BlockSpec(shape, lambda i: (0,) * len(shape))
    flops = 2 * terms * rows * depth * held * outer * (depth + made)
    return pl.pallas_call(
        functools.partial(one_two_kernel, outer, terms, step_rows),
        grid=(rows // step_rows,),
        in_specs=[piece] * (2 * outer - 1) + [whole(first.shape), whole(third.shape)],
        out_specs=pl.BlockSpec((terms, step_rows, made, depth), lambda i: (0, i, 0, 0)),
        out_shape=jax.ShapeDtypeStruct((terms, rows, made, depth), jnp.bfloat16),
        compiler_params=pltpu.CompilerParams(vmem_limit_bytes=48 * MIB),
        cost_estimate=pl.CostEstimate(
            flops=flops,
            bytes_accessed=2 * rows * depth * (held * (2 * outer - 1) + terms * made),
            transcendentals=0,
        ),
        name="third_first",
    )(own, *ups, *downs, first, third)


def final_kernel(pieces, *refs):
    own = refs[:pieces]
    other = refs[pieces : 2 * pieces]
    second_ref, core_ref, out_ref = refs[2 * pieces :]
    for row in range(core_ref.shape[0]):
        parts = [ref[term, row] for term in range(own[0].shape[0]) for ref in own]
        parts += [ref[0, row] for ref in other]
        stacked = jnp.concatenate(parts, axis=0)
        applied = jnp.dot(second_ref[...], stacked, preferred_element_type=jnp.float32)
        out_ref[row] = core_ref[row].astype(jnp.float32) - 0.5 * applied


def final(own, other, second, core):
    rows, count, depth = core.shape
    near = own[0].shape[0]
    chunk = own[0].shape[2]
    step = 2
    flops = 2 * rows * count * second.shape[1] * depth
    return pl.pallas_call(
        functools.partial(final_kernel, len(own)),
        grid=(rows // step,),
        in_specs=[pl.BlockSpec((near, step, chunk, depth), lambda i: (0, i, 0, 0))] * len(own)
        + [pl.BlockSpec((1, step, chunk, depth), lambda i: (0, i, 0, 0))] * len(other)
        + [
            pl.BlockSpec(second.shape, lambda i: (0, 0)),
            pl.BlockSpec((step, count, depth), lambda i: (i, 0, 0)),
        ],
        out_specs=pl.BlockSpec((step, count, depth), lambda i: (i, 0, 0)),
        out_shape=jax.ShapeDtypeStruct((rows, count, depth), jnp.float32),
        compiler_params=pltpu.CompilerParams(vmem_limit_bytes=40 * MIB),
        cost_estimate=pl.CostEstimate(
            flops=flops,
            bytes_accessed=rows * depth * (2 * second.shape[1] + 6 * count),
            transcendentals=0,
        ),
        name="second_final",
    )(*own, *other, second, core)


def shards(core, op_one, op_two, op_three):
    own_core = core[0]
    rows, count, depth = own_core.shape
    terms = op_one.shape[1]
    states = lax.axis_size("state")
    modes = lax.axis_size("mode")
    outer = 4 if modes % 4 == 0 else 1
    inner = modes // outer
    share = count // inner
    chunk = min(share, CHUNK_ROWS)
    state = lax.axis_index("state")
    mode = lax.axis_index("mode")
    place, member = mode // inner, mode % inner

    partner = lambda who, d: who ^ d
    own_first = lax.dynamic_index_in_dim(op_one, state, 0, keepdims=False)
    own_third = lax.dynamic_index_in_dim(op_three, state, 0, keepdims=False)
    own_second = lax.dynamic_index_in_dim(op_two, state, 0, keepdims=False)
    other_second = lax.dynamic_index_in_dim(op_two, states - 1 - state, 0, keepdims=False)

    spot = jnp.arange(modes * rows, dtype=jnp.int32)
    held_place = (place - spot // (inner * rows) + outer) % outer
    held_member = ((spot // rows) % inner) ^ member
    held = (held_place * inner + held_member) * rows + spot % rows
    select = (held[:, None] == spot[None, :]).astype(jnp.bfloat16)
    picked = jnp.einsum("qa,tab->tqb", select[: inner * rows], own_first).astype(jnp.bfloat16)
    first = jnp.einsum("tqb,pb->tqp", picked, select).astype(jnp.bfloat16)
    third = jnp.swapaxes(own_third, 1, 2)

    def columns(matrix):
        return [
            lax.dynamic_slice_in_dim(matrix, partner(member, d) * share, share, 1)
            for d in range(inner)
        ]

    def ordered(matrix):
        return [
            block[:, start : start + chunk]
            for start in range(0, share, chunk)
            for block in columns(matrix)
        ]

    second = []
    for term in range(terms - 1):
        second += ordered(own_second[term])
    second += ordered(other_second[terms - 1])
    second = jnp.concatenate(second, axis=1)

    turned = jnp.swapaxes(own_core, 0, 1)

    def exchange(value, d):
        return lax.ppermute(
            value,
            "mode",
            [
                (z * inner + h, z * inner + partner(h, d))
                for z in range(outer)
                for h in range(inner)
            ],
        )

    def crossed(value, d):
        return lax.ppermute(
            value,
            ("state", "mode"),
            [
                (s * modes + z * inner + h, (states - 1 - s) * modes + z * inner + partner(h, d))
                for s in range(states)
                for z in range(outer)
                for h in range(inner)
            ],
        )

    def relay(value, hop, way):
        pairs = []
        for z in range(outer):
            if 0 <= z + way < outer and 0 <= z - way * (hop - 1) < outer:
                pairs += [(z * inner + h, (z + way) * inner + h) for h in range(inner)]
        return lax.ppermute(value, "mode", pairs)

    near, far = [], []
    for start in range(0, share, chunk):
        pieces = []
        for d in range(inner):
            piece = lax.dynamic_slice_in_dim(turned, partner(member, d) * share + start, chunk, 0)
            pieces.append(exchange(piece, d) if d else piece)
        own = jnp.concatenate(pieces, axis=1)
        ups, downs = [], []
        up = down = own
        for hop in range(1, outer):
            up, down = relay(up, hop, 1), relay(down, hop, -1)
            ups.append(up)
            downs.append(down)
        made = one_three(own, ups, downs, first, third)
        made = made.reshape(terms, chunk, inner, rows, depth)
        for d in range(inner):
            part = jnp.swapaxes(made[:, :, d], 1, 2)
            near.append(exchange(part[:-1], d) if d else part[:-1])
            far.append(crossed(part[-1:], d))
    return final(near, far, second, own_core)[None]


def solution(mesh):
    placed = (P("state", "mode", None, None), P(), P(), P())
    return jax.shard_map(
        shards,
        mesh=mesh,
        in_specs=placed,
        out_specs=P("state", "mode", None, None),
        check_vma=False,
    )
```

time: 1030 us -> 963 us (0.935); the launches traced: 1030 us -> 946 us
  blocking collectives: 187 us -> 0 us
  Pallas kernels: 0 us -> 175 us
  matrix products: 75.8 us -> 2.42 us
  waiting for transfers between devices: 614 us -> 577 us
  starting transfers between devices: 42.1 us -> 78.6 us
  local copies, waits for them, and re-layouts: 87.8 us -> 110 us
  other arithmetic: 22.2 us -> 1.63 us
    all_to_all x3 -> x0, waiting for transfers between devices: 429 us -> none  [shards(): lax.all_to_all(prepared[term], 'mode', split_axis=1, concat_axis=0, tiled...]
    ppermute x1 -> x64, waiting for transfers between devices: 185 us -> 577 us  [the longest x24 352 us: relay(): return lax.ppermute(value, 'mode', pairs)]
    all_to_all x1 -> x0, blocking collectives: 187 us -> none  [shards(): lax.all_to_all(applied, 'mode', split_axis=0, concat_axis=1, tiled=True)]
    pallas_call x0 -> x5, Pallas kernels: none -> 175 us  [the longest x4 151 us: one_three(): pl.pallas_call(functools.partial(one_two_kernel, outer, terms, step_rows)...]
    ppermute x1 -> x64, starting transfers between devices: 1.49 us -> 78.6 us  [the longest x24 41.3 us: relay(): return lax.ppermute(value, 'mode', pairs)]
    dot_general x6 -> x1, matrix products: 75.8 us -> 2.42 us  [shards(): first = jnp.einsum('tqb,pb->tqp', picked, select).astype(jnp.bfloat16)]
    convert_element_type x4 -> x0, local copies, waits for them, and re-layouts: 55.2 us -> none  [the longest x3 43.8 us: mode_two_three(): jnp.einsum('ab,ibk->iak', second, inner, preferred_element_type=jnp.float32)]
    slice x0 -> x42, local copies, waits for them, and re-layouts: none -> 47.4 us  [the longest x16 20 us: shards(): near.append(exchange(part[:-1], d) if d else part[:-1])]
  transfers between devices with their start and end apart: 4 -> 64, of which waited for: 4 -> 33; matrix products, arithmetic and copies ran while one was open for 10% -> 9% of each run, Pallas kernels for 0% -> 16%
where the time goes in v1:
time: 963 us; the launch traced here: 946 us
  waiting for transfers between devices  577 us (60%)
  Pallas kernels  175 us (18%)
  local copies, waits for them, and re-layouts  110 us (11%)
  starting transfers between devices  78.6 us (8%)
    ppermute x24, waiting for transfers between devices, relay(): return lax.ppermute(value, 'mode', pairs)  352 us
    ppermute x24, waiting for transfers between devices, exchange(): lax.ppermute(value, 'mode', [(z * inner + h, z * inner + partner(h, d)) f...  176 us
    pallas_call x4, Pallas kernels, one_three(): pl.pallas_call(functools.partial(one_two_kernel, outer, terms, step_rows)...  151 us
    ppermute x16, waiting for transfers between devices, crossed(): lax.ppermute(value, ('state', 'mode'), [(s * modes + z * inner + h, (stat...  49.6 us
    unnamed x192, local copies, waits for them, and re-layouts  41.4 us
    ppermute x24, starting transfers between devices, relay(): return lax.ppermute(value, 'mode', pairs)  41.3 us
    pallas_call x1, Pallas kernels, final(): pl.pallas_call(functools.partial(final_kernel, len(own)), grid=(rows // s...  24.1 us
    ppermute x24, starting transfers between devices, exchange(): lax.ppermute(value, 'mode', [(z * inner + h, z * inner + partner(h, d)) f...  21.8 us
  transfers between devices with their start and end apart: 64, of which 33 were waited for; matrix products, arithmetic and copies ran while one was open for 9% of the time, Pallas kernels for 16%

profile of v1, /device:TPU:24, one launch (start us, length us, event | category | flops | bytes accessed | tf_op | source)
XLA Modules:
  0.0 946.3 jit_solution(1649802292883442680)
XLA Ops:
  0.0 4.6 constant_dynamic-slice_fusion.3
  10.4 8.7 collective-permute-done.38
  21.8 8.7 collective-permute-done.25
  32.9 8.9 collective-permute-done.37
  43.4 9.4 collective-permute-done.26
  52.8 2.5 collective-permute-start.42
  56.8 7.4 collective-permute-done.1
  64.2 2.5 collective-permute-start.30
  68.3 7.1 collective-permute-done.13
  76.9 12.5 %collective-permute-done.14 = bf16[32,32,256]{2,1,0:T(8,128)(2,1)S(1)} collective-permute-done((bf16[32,32,256]{2,1,0:T(8,128)(2,1)S(1)}, bf16[32,32,256]{2,1,0:T(8,128)(2,1)S(1)}, u32[]{:S(2)}, u32[]{:S(2)}) %collective-permute-start.14) | collective-permute-done | bytes 524320 | tf_op jit(solution)/shard_map/ppermute | solution.py:153
  91.4 11.8 %collective-permute-done.2 = bf16[32,32,256]{2,1,0:T(8,128)(2,1)S(1)} collective-permute-done((bf16[32,32,256]{2,1,0:T(8,128)(2,1)S(1)}, bf16[32,32,256]{2,1,0:T(8,128)(2,1)S(1)}, u32[]{:S(2)}, u32[]{:S(2)}) %collective-permute-start.2) | collective-permute-done | bytes 524320 | tf_op jit(solution)/shard_map/ppermute | solution.py:153
  103.2 2.5 collective-permute-start.18
  107.5 4.7 collective-permute-start.6
  112.2 34.0 %collective-permute-done.30.refs_4_ = bf16[32,128,256]{2,1,0:T(8,128)(2,1)S(1)} collective-permute-done((bf16[32,128,256]{2,1,0:T(8,128)(2,1)S(1)}, bf16[32,128,256]{2,1,0:T(8,128)(2,1)S(1)}, u32[]{:S(2)}, u32[]{:S(2)}) %collective-permute-start.30) | collective-permute-done | bytes 2097184 | tf_op jit(solution)/shard_map/ppermute | solution.py:180
  152.9 38.2 %collective-permute-done.18.refs_4_ = bf16[32,128,256]{2,1,0:T(8,128)(2,1)S(1)} collective-permute-done((bf16[32,128,256]{2,1,0:T(8,128)(2,1)S(1)}, bf16[32,128,256]{2,1,0:T(8,128)(2,1)S(1)}, u32[]{:S(2)}, u32[]{:S(2)}) %collective-permute-start.18) | collective-permute-done | bytes 2097184 | tf_op jit(solution)/shard_map/ppermute | solution.py:180
  197.8 37.4 %collective-permute-done.6.refs_4_ = bf16[32,128,256]{2,1,0:T(8,128)(2,1)S(1)} collective-permute-done((bf16[32,128,256]{2,1,0:T(8,128)(2,1)S(1)}, bf16[32,128,256]{2,1,0:T(8,128)(2,1)S(1)}, u32[]{:S(2)}, u32[]{:S(2)}) %collective-permute-start.6) | collective-permute-done | bytes 2097184 | tf_op jit(solution)/shard_map/ppermute | solution.py:180
  237.8 3.1 collective-permute-done.3.refs_1_
  244.3 41.5 %collective-permute-done.40.refs_2_ = bf16[32,128,256]{2,1,0:T(8,128)(2,1)} collective-permute-done((bf16[32,128,256]{2,1,0:T(8,128)(2,1)S(1)}, bf16[32,128,256]{2,1,0:T(8,128)(2,1)}, u32[]{:S(2)}, u32[]{:S(2)}) %collective-permute-start.40) | collective-permute-done | bytes 2097184 | tf_op jit(solution)/shard_map/ppermute | solution.py:180
  287.9 42.8 %collective-permute-done.28.refs_2_ = bf16[32,128,256]{2,1,0:T(8,128)(2,1)} collective-permute-done((bf16[32,128,256]{2,1,0:T(8,128)(2,1)S(1)}, bf16[32,128,256]{2,1,0:T(8,128)(2,1)}, u32[]{:S(2)}, u32[]{:S(2)}) %collective-permute-start.28) | collective-permute-done | bytes 2097184 | tf_op jit(solution)/shard_map/ppermute | solution.py:180
  334.3 41.3 %collective-permute-done.16.refs_2_ = bf16[32,128,256]{2,1,0:T(8,128)(2,1)S(1)} collective-permute-done((bf16[32,128,256]{2,1,0:T(8,128)(2,1)S(1)}, bf16[32,128,256]{2,1,0:T(8,128)(2,1)S(1)}, u32[]{:S(2)}, u32[]{:S(2)}) %collective-permute-start.16) | collective-permute-done | bytes 2097184 | tf_op jit(solution)/shard_map/ppermute | solution.py:180
  384.2 2.4 fusion.7.refs_7_
  386.7 34.0 %collective-permute-done.4.refs_2_ = bf16[32,128,256]{2,1,0:T(8,128)(2,1)} collective-permute-done((bf16[32,128,256]{2,1,0:T(8,128)(2,1)}, bf16[32,128,256]{2,1,0:T(8,128)(2,1)}, u32[]{:S(2)}, u32[]{:S(2)}) %collective-permute-start.4) | collective-permute-done | bytes 2097184 | tf_op jit(solution)/shard_map/ppermute | solution.py:180
  423.9 41.6 %collective-permute-done.41.refs_3_ = bf16[32,128,256]{2,1,0:T(8,128)(2,1)} collective-permute-done((bf16[32,128,256]{2,1,0:T(8,128)(2,1)}, bf16[32,128,256]{2,1,0:T(8,128)(2,1)}, u32[]{:S(2)}, u32[]{:S(2)}) %collective-permute-start.41) | collective-permute-done | bytes 2097184 | tf_op jit(solution)/shard_map/ppermute | solution.py:180
  473.0 35.3 %third_first.7 = bf16[3,32,128,256]{3,2,1,0:T(8,128)(2,1)} custom-call(bf16[32,128,256]{2,1,0:T(8,128)(2,1)S(1)} %copy-done.9, bf16[32,128,256]{2,1,0:T(8,128)(2,1)S(1)} %copy-done.53, bf16[32,128,256]{2,1,0:T(8,128)(2,1)} %collective-permute-done.40.refs_2_, bf16[32,128,256]{2,1,0:T(8,128)(2,1)} %collective-permute-done.41.refs_3_, ...), custom_call_target="tpu_custom_call" | custom-call | flops 9663676416 | bytes 20971520 | tf_op jit(solution)/shard_map/third_first/pallas_call | solution.py:47
  508.3 3.6 fusion.27
  519.4 35.3 %third_first.6 = bf16[3,32,128,256]{3,2,1,0:T(8,128)(2,1)} custom-call(bf16[32,128,256]{2,1,0:T(8,128)(2,1)S(1)} %copy-done.5, bf16[32,128,256]{2,1,0:T(8,128)(2,1)S(1)} %copy-done.49, bf16[32,128,256]{2,1,0:T(8,128)(2,1)} %collective-permute-done.28.refs_2_, bf16[32,128,256]{2,1,0:T(8,128)(2,1)} %collective-permute-done.29.refs_3_, ...), custom_call_target="tpu_custom_call" | custom-call | flops 9663676416 | bytes 20971520 | tf_op jit(solution)/shard_map/third_first/pallas_call | solution.py:47
  554.7 5.2 fusion.28
  561.6 2.5 collective-permute-start.62
  565.3 34.0 %collective-permute-done.5.refs_3_ = bf16[32,128,256]{2,1,0:T(8,128)(2,1)} collective-permute-done((bf16[32,128,256]{2,1,0:T(8,128)(2,1)}, bf16[32,128,256]{2,1,0:T(8,128)(2,1)}, u32[]{:S(2)}, u32[]{:S(2)}) %collective-permute-start.5) | collective-permute-done | bytes 2097184 | tf_op jit(solution)/shard_map/ppermute | solution.py:180
  600.3 35.3 %third_first.5 = bf16[3,32,128,256]{3,2,1,0:T(8,128)(2,1)} custom-call(bf16[32,128,256]{2,1,0:T(8,128)(2,1)S(1)} %copy-done.7, bf16[32,128,256]{2,1,0:T(8,128)(2,1)S(1)} %copy-done.51, bf16[32,128,256]{2,1,0:T(8,128)(2,1)} %copy-done.85, bf16[32,128,256]{2,1,0:T(8,128)(2,1)} %collective-permute-done.17.refs_3_, bf16[32,128,256]{2,1,0:T(8,128)(2,1)} %copy-done.80, ...), custom_call_target="tpu_custom_call" | custom-call | flops 9663676416 | bytes 20971520 | tf_op jit(solution)/shard_map/third_first/pallas_call | solution.py:47
  635.6 2.4 copy.108
  655.4 44.6 %third_first.4 = bf16[3,32,128,256]{3,2,1,0:T(8,128)(2,1)} custom-call(bf16[32,128,256]{2,1,0:T(8,128)(2,1)S(1)} %copy-done.3, bf16[32,128,256]{2,1,0:T(8,128)(2,1)} %collective-permute-done.3.refs_1_, bf16[32,128,256]{2,1,0:T(8,128)(2,1)} %collective-permute-done.4.refs_2_, bf16[32,128,256]{2,1,0:T(8,128)(2,1)} %collective-permute-done.5.refs_3_, ...), custom_call_target="tpu_custom_call" | custom-call | flops 9663676416 | bytes 20971520 | tf_op jit(solution)/shard_map/third_first/pallas_call | solution.py:47
  717.8 3.4 collective-permute-done.53.refs_21_
  722.3 10.7 %collective-permute-done.52.refs_20_ = bf16[1,32,32,256]{3,2,1,0:T(8,128)(2,1)S(1)} collective-permute-done((bf16[1,32,32,256]{3,2,1,0:T(8,128)(2,1)S(1)}, bf16[1,32,32,256]{3,2,1,0:T(8,128)(2,1)S(1)}, u32[]{:S(2)}, u32[]{:S(2)}) %collective-permute-start.52) | collective-permute-done | bytes 524320 | tf_op jit(solution)/shard_map/ppermute | solution.py:164
  732.9 10.8 %collective-permute-done.51.refs_19_ = bf16[1,32,32,256]{3,2,1,0:T(8,128)(2,1)S(1)} collective-permute-done((bf16[1,32,32,256]{3,2,1,0:T(8,128)(2,1)S(1)}, bf16[1,32,32,256]{3,2,1,0:T(8,128)(2,1)S(1)}, u32[]{:S(2)}, u32[]{:S(2)}) %collective-permute-start.51) | collective-permute-done | bytes 524320 | tf_op jit(solution)/shard_map/ppermute | solution.py:164
  749.3 7.2 collective-permute-done.50.refs_18_
  757.3 8.8 collective-permute-done.49.refs_17_
  768.9 8.7 collective-permute-done.48.refs_16_
  779.6 3.0 collective-permute-done.46.refs_14_
  791.0 11.9 %collective-permute-done.35.refs_11_ = bf16[2,32,32,256]{3,2,1,0:T(8,128)(2,1)} collective-permute-done((bf16[2,32,32,256]{3,2,1,0:T(8,128)(2,1)}, bf16[2,32,32,256]{3,2,1,0:T(8,128)(2,1)}, u32[]{:S(2)}, u32[]{:S(2)}) %collective-permute-start.35) | collective-permute-done | bytes 1048608 | tf_op jit(solution)/shard_map/ppermute | solution.py:153
  804.8 22.6 %collective-permute-done.34.refs_10_ = bf16[2,32,32,256]{3,2,1,0:T(8,128)(2,1)} collective-permute-done((bf16[2,32,32,256]{3,2,1,0:T(8,128)(2,1)}, bf16[2,32,32,256]{3,2,1,0:T(8,128)(2,1)}, u32[]{:S(2)}, u32[]{:S(2)}) %collective-permute-start.34) | collective-permute-done | bytes 1048608 | tf_op jit(solution)/shard_map/ppermute | solution.py:153
  827.9 20.0 %collective-permute-done.23.refs_7_ = bf16[2,32,32,256]{3,2,1,0:T(8,128)(2,1)} collective-permute-done((bf16[2,32,32,256]{3,2,1,0:T(8,128)(2,1)}, bf16[2,32,32,256]{3,2,1,0:T(8,128)(2,1)}, u32[]{:S(2)}, u32[]{:S(2)}) %collective-permute-start.23) | collective-permute-done | bytes 1048608 | tf_op jit(solution)/shard_map/ppermute | solution.py:153
  856.0 7.3 concatenate.19.refs_32_
  863.4 2.5 slice.429.refs_12_
  865.9 2.5 slice.421.refs_8_
  872.4 20.4 %collective-permute-done.11.refs_3_ = bf16[2,32,32,256]{3,2,1,0:T(8,128)(2,1)S(1)} collective-permute-done((bf16[2,32,32,256]{3,2,1,0:T(8,128)(2,1)}, bf16[2,32,32,256]{3,2,1,0:T(8,128)(2,1)S(1)}, u32[]{:S(2)}, u32[]{:S(2)}) %collective-permute-start.11) | collective-permute-done | bytes 1048608 | tf_op jit(solution)/shard_map/ppermute | solution.py:153
  893.8 22.4 %collective-permute-done.10.refs_2_ = bf16[2,32,32,256]{3,2,1,0:T(8,128)(2,1)S(1)} collective-permute-done((bf16[2,32,32,256]{3,2,1,0:T(8,128)(2,1)}, bf16[2,32,32,256]{3,2,1,0:T(8,128)(2,1)S(1)}, u32[]{:S(2)}, u32[]{:S(2)}) %collective-permute-start.10) | collective-permute-done | bytes 1048608 | tf_op jit(solution)/shard_map/ppermute | solution.py:153
  922.0 24.1 %second_final.1 = f32[32,512,256]{2,1,0:T(8,128)} custom-call(bf16[2,32,32,256]{3,2,1,0:T(8,128)(2,1)S(1)} %slice.405.refs_0_, bf16[2,32,32,256]{3,2,1,0:T(8,128)(2,1)S(1)} %copy-done.15, bf16[2,32,32,256]{3,2,1,0:T(8,128)(2,1)S(1)} %copy-done.13, bf16[2,32,32,256]{3,2,1,0:T(8,128)(2,1)S(1)} %copy-done.11, bf16[2,32,32,256]{3,2,1,0:T(8,128)(2,1)S(1)} %slice.413.refs_4_, ...), custom_call_target="tpu_custom_call" | custom-call | flops 12884901888 | bytes 50331648 | tf_op jit(solution)/shard_map/second_final/pallas_call | solution.py:81
  (348 shorter events, 152.9 us)
Async XLA Ops:
  32.0 34.7 %collective-permute-start.12 = (bf16[32,32,256]{2,1,0:T(8,128)(2,1)S(1)}, bf16[32,32,256]{2,1,0:T(8,128)(2,1)S(1)}, u32[]{:S(2)}, u32[]{:S(2)}) collective-permute-start(bf16[32,32,256]{2,1,0:T(8,128)(2,1)S(1)} %bitcast.258), channel_id=1, source_target_pairs={{0,1},{1,0},{2,3},{3,2},{4,5},{5,4},{6,7},{7,6},{8,9},{9,8},{10,11... | collective-permute-start | bytes 1572872 | tf_op jit(solution)/shard_map/ppermute | solution.py:153
  52.8 53.3 %collective-permute-start.42 = (bf16[32,128,256]{2,1,0:T(8,128)(2,1)S(1)}, bf16[32,128,256]{2,1,0:T(8,128)(2,1)S(1)}, u32[]{:S(2)}, u32[]{:S(2)}) collective-permute-start(bf16[32,128,256]{2,1,0:T(8,128)(2,1)S(1)} %pad_maximum_fusion.3.refs_0_), channel_id=1, source_target_pairs={{4,0},{5,1},{6,2},{7,3},{8,4},{9,5},{10,6},{11,7},{12,8},{13,9},{1... | collective-permute-start | bytes 6291464 | tf_op jit(solution)/shard_map/ppermute | solution.py:180
  55.5 51.9 %collective-permute-start.39 = (bf16[32,128,256]{2,1,0:T(8,128)(2,1)S(1)}, bf16[32,128,256]{2,1,0:T(8,128)(2,1)S(1)}, u32[]{:S(2)}, u32[]{:S(2)}) collective-permute-start(bf16[32,128,256]{2,1,0:T(8,128)(2,1)S(1)} %pad_maximum_fusion.3.refs_0_), channel_id=1, source_target_pairs={{0,4},{1,5},{2,6},{3,7},{4,8},{5,9},{6,10},{7,11},{8,12},{9,13},{1... | collective-permute-start | bytes 6291464 | tf_op jit(solution)/shard_map/ppermute | solution.py:180
  64.2 81.9 %collective-permute-start.30 = (bf16[32,128,256]{2,1,0:T(8,128)(2,1)S(1)}, bf16[32,128,256]{2,1,0:T(8,128)(2,1)S(1)}, u32[]{:S(2)}, u32[]{:S(2)}) collective-permute-start(bf16[32,128,256]{2,1,0:T(8,128)(2,1)S(1)} %pad_maximum_fusion.2.refs_0_), channel_id=1, source_target_pairs={{4,0},{5,1},{6,2},{7,3},{8,4},{9,5},{10,6},{11,7},{12,8},{13,9},{1... | collective-permute-start | bytes 6291464 | tf_op jit(solution)/shard_map/ppermute | solution.py:180
  66.7 84.2 %collective-permute-start.27 = (bf16[32,128,256]{2,1,0:T(8,128)(2,1)S(1)}, bf16[32,128,256]{2,1,0:T(8,128)(2,1)S(1)}, u32[]{:S(2)}, u32[]{:S(2)}) collective-permute-start(bf16[32,128,256]{2,1,0:T(8,128)(2,1)S(1)} %pad_maximum_fusion.2.refs_0_), channel_id=1, source_target_pairs={{0,4},{1,5},{2,6},{3,7},{4,8},{5,9},{6,10},{7,11},{8,12},{9,13},{1... | collective-permute-start | bytes 6291464 | tf_op jit(solution)/shard_map/ppermute | solution.py:180
  103.2 87.9 %collective-permute-start.18 = (bf16[32,128,256]{2,1,0:T(8,128)(2,1)S(1)}, bf16[32,128,256]{2,1,0:T(8,128)(2,1)S(1)}, u32[]{:S(2)}, u32[]{:S(2)}) collective-permute-start(bf16[32,128,256]{2,1,0:T(8,128)(2,1)S(1)} %pad_maximum_fusion.1.refs_0_), channel_id=1, source_target_pairs={{4,0},{5,1},{6,2},{7,3},{8,4},{9,5},{10,6},{11,7},{12,8},{13,9},{1... | collective-permute-start | bytes 6291464 | tf_op jit(solution)/shard_map/ppermute | solution.py:180
  106.2 89.7 %collective-permute-start.15 = (bf16[32,128,256]{2,1,0:T(8,128)(2,1)S(1)}, bf16[32,128,256]{2,1,0:T(8,128)(2,1)S(1)}, u32[]{:S(2)}, u32[]{:S(2)}) collective-permute-start(bf16[32,128,256]{2,1,0:T(8,128)(2,1)S(1)} %pad_maximum_fusion.1.refs_0_), channel_id=1, source_target_pairs={{0,4},{1,5},{2,6},{3,7},{4,8},{5,9},{6,10},{7,11},{8,12},{9,13},{1... | collective-permute-start | bytes 6291464 | tf_op jit(solution)/shard_map/ppermute | solution.py:180
  107.5 127.7 %collective-permute-start.6 = (bf16[32,128,256]{2,1,0:T(8,128)(2,1)S(1)}, bf16[32,128,256]{2,1,0:T(8,128)(2,1)S(1)}, u32[]{:S(2)}, u32[]{:S(2)}) collective-permute-start(bf16[32,128,256]{2,1,0:T(8,128)(2,1)S(1)} %pad_maximum_fusion.refs_0_), channel_id=1, source_target_pairs={{4,0},{5,1},{6,2},{7,3},{8,4},{9,5},{10,6},{11,7},{12,8},{13,9},{1... | collective-permute-start | bytes 6291464 | tf_op jit(solution)/shard_map/ppermute | solution.py:180
  146.1 94.8 %collective-permute-start.3 = (bf16[32,128,256]{2,1,0:T(8,128)(2,1)S(1)}, bf16[32,128,256]{2,1,0:T(8,128)(2,1)}, u32[]{:S(2)}, u32[]{:S(2)}) collective-permute-start(bf16[32,128,256]{2,1,0:T(8,128)(2,1)S(1)} %pad_maximum_fusion.refs_0_), channel_id=1, source_target_pairs={{0,4},{1,5},{2,6},{3,7},{4,8},{5,9},{6,10},{7,11},{8,12},{9,13},{1... | collective-permute-start | bytes 6291464 | tf_op jit(solution)/shard_map/ppermute | solution.py:180
  150.9 90.8 %collective-permute-start.43 = (bf16[32,128,256]{2,1,0:T(8,128)(2,1)S(1)}, bf16[32,128,256]{2,1,0:T(8,128)(2,1)}, u32[]{:S(2)}, u32[]{:S(2)}) collective-permute-start(bf16[32,128,256]{2,1,0:T(8,128)(2,1)S(1)} %collective-permute-done.42.refs_4_), channel_id=1, source_target_pairs={{4,0},{5,1},{6,2},{7,3},{8,4},{9,5},{10,6},{11,7},{20,16},{21,17},... | collective-permute-start | bytes 6291464 | tf_op jit(solution)/shard_map/ppermute | solution.py:180
  191.0 94.8 %collective-permute-start.40 = (bf16[32,128,256]{2,1,0:T(8,128)(2,1)S(1)}, bf16[32,128,256]{2,1,0:T(8,128)(2,1)}, u32[]{:S(2)}, u32[]{:S(2)}) collective-permute-start(bf16[32,128,256]{2,1,0:T(8,128)(2,1)S(1)} %collective-permute-done.39.refs_1_), channel_id=1, source_target_pairs={{4,8},{5,9},{6,10},{7,11},{8,12},{9,13},{10,14},{11,15},{20,24},{2... | collective-permute-start | bytes 6291464 | tf_op jit(solution)/shard_map/ppermute | solution.py:180
  195.8 90.8 %collective-permute-start.31 = (bf16[32,128,256]{2,1,0:T(8,128)(2,1)S(1)}, bf16[32,128,256]{2,1,0:T(8,128)(2,1)}, u32[]{:S(2)}, u32[]{:S(2)}) collective-permute-start(bf16[32,128,256]{2,1,0:T(8,128)(2,1)S(1)} %collective-permute-done.30.refs_4_), channel_id=1, source_target_pairs={{4,0},{5,1},{6,2},{7,3},{8,4},{9,5},{10,6},{11,7},{20,16},{21,17},... | collective-permute-start | bytes 6291464 | tf_op jit(solution)/shard_map/ppermute | solution.py:180
  235.2 95.6 %collective-permute-start.28 = (bf16[32,128,256]{2,1,0:T(8,128)(2,1)S(1)}, bf16[32,128,256]{2,1,0:T(8,128)(2,1)}, u32[]{:S(2)}, u32[]{:S(2)}) collective-permute-start(bf16[32,128,256]{2,1,0:T(8,128)(2,1)S(1)} %collective-permute-done.27.refs_1_), channel_id=1, source_target_pairs={{4,8},{5,9},{6,10},{7,11},{8,12},{9,13},{10,14},{11,15},{20,24},{2... | collective-permute-start | bytes 6291464 | tf_op jit(solution)/shard_map/ppermute | solution.py:180
  240.9 92.1 %collective-permute-start.19 = (bf16[32,128,256]{2,1,0:T(8,128)(2,1)S(1)}, bf16[32,128,256]{2,1,0:T(8,128)(2,1)S(1)}, u32[]{:S(2)}, u32[]{:S(2)}) collective-permute-start(bf16[32,128,256]{2,1,0:T(8,128)(2,1)S(1)} %collective-permute-done.18.refs_4_), channel_id=1, source_target_pairs={{4,0},{5,1},{6,2},{7,3},{8,4},{9,5},{10,6},{11,7},{20,16},{21,17},... | collective-permute-start | bytes 6291464 | tf_op jit(solution)/shard_map/ppermute | solution.py:180
  241.7 133.9 %collective-permute-start.16 = (bf16[32,128,256]{2,1,0:T(8,128)(2,1)S(1)}, bf16[32,128,256]{2,1,0:T(8,128)(2,1)S(1)}, u32[]{:S(2)}, u32[]{:S(2)}) collective-permute-start(bf16[32,128,256]{2,1,0:T(8,128)(2,1)S(1)} %collective-permute-done.15.refs_1_), channel_id=1, source_target_pairs={{4,8},{5,9},{6,10},{7,11},{8,12},{9,13},{10,14},{11,15},{20,24},{2... | collective-permute-start | bytes 6291464 | tf_op jit(solution)/shard_map/ppermute | solution.py:180
  285.8 91.8 %collective-permute-start.7 = (bf16[32,128,256]{2,1,0:T(8,128)(2,1)S(1)}, bf16[32,128,256]{2,1,0:T(8,128)(2,1)S(1)}, u32[]{:S(2)}, u32[]{:S(2)}) collective-permute-start(bf16[32,128,256]{2,1,0:T(8,128)(2,1)S(1)} %collective-permute-done.6.refs_4_), channel_id=1, source_target_pairs={{4,0},{5,1},{6,2},{7,3},{8,4},{9,5},{10,6},{11,7},{20,16},{21,17},... | collective-permute-start | bytes 6291464 | tf_op jit(solution)/shard_map/ppermute | solution.py:180
  286.6 134.0 %collective-permute-start.4 = (bf16[32,128,256]{2,1,0:T(8,128)(2,1)}, bf16[32,128,256]{2,1,0:T(8,128)(2,1)}, u32[]{:S(2)}, u32[]{:S(2)}) collective-permute-start(bf16[32,128,256]{2,1,0:T(8,128)(2,1)} %collective-permute-done.3.refs_1_), channel_id=1, source_target_pairs={{4,8},{5,9},{6,10},{7,11},{8,12},{9,13},{10,14},{11,15},{20,24},{2... | collective-permute-start | bytes 6291464 | tf_op jit(solution)/shard_map/ppermute | solution.py:180
  330.7 91.9 %collective-permute-start.44 = (bf16[32,128,256]{2,1,0:T(8,128)(2,1)}, bf16[32,128,256]{2,1,0:T(8,128)(2,1)}, u32[]{:S(2)}, u32[]{:S(2)}) collective-permute-start(bf16[32,128,256]{2,1,0:T(8,128)(2,1)} %collective-permute-done.43.refs_5_), channel_id=1, source_target_pairs={{4,0},{5,1},{6,2},{7,3},{20,16},{21,17},{22,18},{23,19}} | collective-permute-start | bytes 6291464 | tf_op jit(solution)/shard_map/ppermute | solution.py:180
  333.0 132.6 %collective-permute-start.41 = (bf16[32,128,256]{2,1,0:T(8,128)(2,1)}, bf16[32,128,256]{2,1,0:T(8,128)(2,1)}, u32[]{:S(2)}, u32[]{:S(2)}) collective-permute-start(bf16[32,128,256]{2,1,0:T(8,128)(2,1)} %collective-permute-done.40.refs_2_), channel_id=1, source_target_pairs={{8,12},{9,13},{10,14},{11,15},{24,28},{25,29},{26,30},{27,31}} | collective-permute-start | bytes 6291464 | tf_op jit(solution)/shard_map/ppermute | solution.py:180
  375.6 91.9 %collective-permute-start.32 = (bf16[32,128,256]{2,1,0:T(8,128)(2,1)}, bf16[32,128,256]{2,1,0:T(8,128)(2,1)}, u32[]{:S(2)}, u32[]{:S(2)}) collective-permute-start(bf16[32,128,256]{2,1,0:T(8,128)(2,1)} %collective-permute-done.31.refs_5_), channel_id=1, source_target_pairs={{4,0},{5,1},{6,2},{7,3},{20,16},{21,17},{22,18},{23,19}} | collective-permute-start | bytes 6291464 | tf_op jit(solution)/shard_map/ppermute | solution.py:180
  379.0 139.6 %collective-permute-start.29 = (bf16[32,128,256]{2,1,0:T(8,128)(2,1)}, bf16[32,128,256]{2,1,0:T(8,128)(2,1)}, u32[]{:S(2)}, u32[]{:S(2)}) collective-permute-start(bf16[32,128,256]{2,1,0:T(8,128)(2,1)} %collective-permute-done.28.refs_2_), channel_id=1, source_target_pairs={{8,12},{9,13},{10,14},{11,15},{24,28},{25,29},{26,30},{27,31}} | collective-permute-start | bytes 6291464 | tf_op jit(solution)/shard_map/ppermute | solution.py:180
  420.6 141.0 %collective-permute-start.20 = (bf16[32,128,256]{2,1,0:T(8,128)(2,1)}, bf16[32,128,256]{2,1,0:T(8,128)(2,1)}, u32[]{:S(2)}, u32[]{:S(2)}) collective-permute-start(bf16[32,128,256]{2,1,0:T(8,128)(2,1)} %copy-done.84), channel_id=1, source_target_pairs={{4,0},{5,1},{6,2},{7,3},{20,16},{21,17},{22,18},{23,19}} | collective-permute-start | bytes 6291464 | tf_op jit(solution)/shard_map/ppermute | solution.py:180
  422.7 141.5 %collective-permute-start.17 = (bf16[32,128,256]{2,1,0:T(8,128)(2,1)}, bf16[32,128,256]{2,1,0:T(8,128)(2,1)}, u32[]{:S(2)}, u32[]{:S(2)}) collective-permute-start(bf16[32,128,256]{2,1,0:T(8,128)(2,1)} %copy-done.85), channel_id=1, source_target_pairs={{8,12},{9,13},{10,14},{11,15},{24,28},{25,29},{26,30},{27,31}} | collective-permute-start | bytes 6291464 | tf_op jit(solution)/shard_map/ppermute | solution.py:180
  465.6 99.2 %collective-permute-start.8 = (bf16[32,128,256]{2,1,0:T(8,128)(2,1)}, bf16[32,128,256]{2,1,0:T(8,128)(2,1)}, u32[]{:S(2)}, u32[]{:S(2)}) collective-permute-start(bf16[32,128,256]{2,1,0:T(8,128)(2,1)} %copy-done.82), channel_id=1, source_target_pairs={{4,0},{5,1},{6,2},{7,3},{20,16},{21,17},{22,18},{23,19}} | collective-permute-start | bytes 6291464 | tf_op jit(solution)/shard_map/ppermute | solution.py:180
  467.5 131.7 %collective-permute-start.5 = (bf16[32,128,256]{2,1,0:T(8,128)(2,1)}, bf16[32,128,256]{2,1,0:T(8,128)(2,1)}, u32[]{:S(2)}, u32[]{:S(2)}) collective-permute-start(bf16[32,128,256]{2,1,0:T(8,128)(2,1)} %collective-permute-done.4.refs_2_), channel_id=1, source_target_pairs={{8,12},{9,13},{10,14},{11,15},{24,28},{25,29},{26,30},{27,31}} | collective-permute-start | bytes 6291464 | tf_op jit(solution)/shard_map/ppermute | solution.py:180
  518.6 130.8 %collective-permute-start.63 = (bf16[1,32,32,256]{3,2,1,0:T(8,128)(2,1)}, bf16[1,32,32,256]{3,2,1,0:T(8,128)(2,1)S(1)}, u32[]{:S(2)}, u32[]{:S(2)}) collective-permute-start(bf16[1,32,32,256]{3,2,1,0:T(8,128)(2,1)} %slice.451), channel_id=1, source_target_pairs={{0,19},{1,18},{2,17},{3,16},{4,23},{5,22},{6,21},{7,20},{8,27},{9,... | collective-permute-start | bytes 1572872 | tf_op jit(solution)/shard_map/ppermute | solution.py:164
  561.6 89.2 %collective-permute-start.62 = (bf16[1,32,32,256]{3,2,1,0:T(8,128)(2,1)S(1)}, bf16[1,32,32,256]{3,2,1,0:T(8,128)(2,1)S(1)}, u32[]{:S(2)}, u32[]{:S(2)}) collective-permute-start(bf16[1,32,32,256]{3,2,1,0:T(8,128)(2,1)S(1)} %slice.450), channel_id=1, source_target_pairs={{0,18},{1,19},{2,16},{3,17},{4,22},{5,23},{6,20},{7,21},{8,26},{9,... | collective-permute-start | bytes 1572872 | tf_op jit(solution)/shard_map/ppermute | solution.py:164
  564.2 88.0 %collective-permute-start.61 = (bf16[1,32,32,256]{3,2,1,0:T(8,128)(2,1)}, bf16[1,32,32,256]{3,2,1,0:T(8,128)(2,1)S(1)}, u32[]{:S(2)}, u32[]{:S(2)}) collective-permute-start(bf16[1,32,32,256]{3,2,1,0:T(8,128)(2,1)} %slice.449), channel_id=1, source_target_pairs={{0,17},{1,16},{2,19},{3,18},{4,21},{5,20},{6,23},{7,22},{8,25},{9,... | collective-permute-start | bytes 1572872 | tf_op jit(solution)/shard_map/ppermute | solution.py:164
  564.8 88.0 %collective-permute-start.60 = (bf16[1,32,32,256]{3,2,1,0:T(8,128)(2,1)}, bf16[1,32,32,256]{3,2,1,0:T(8,128)(2,1)S(1)}, u32[]{:S(2)}, u32[]{:S(2)}) collective-permute-start(bf16[1,32,32,256]{3,2,1,0:T(8,128)(2,1)} %slice.448), channel_id=1, source_target_pairs={{0,16},{1,17},{2,18},{3,19},{4,20},{5,21},{6,22},{7,23},{8,24},{9,... | collective-permute-start | bytes 1572872 | tf_op jit(solution)/shard_map/ppermute | solution.py:164
  599.2 54.6 %collective-permute-start.59 = (bf16[1,32,32,256]{3,2,1,0:T(8,128)(2,1)}, bf16[1,32,32,256]{3,2,1,0:T(8,128)(2,1)S(1)}, u32[]{:S(2)}, u32[]{:S(2)}) collective-permute-start(bf16[1,32,32,256]{3,2,1,0:T(8,128)(2,1)} %slice.447), channel_id=1, source_target_pairs={{0,19},{1,18},{2,17},{3,16},{4,23},{5,22},{6,21},{7,20},{8,27},{9,... | collective-permute-start | bytes 1572872 | tf_op jit(solution)/shard_map/ppermute | solution.py:164
  649.4 57.7 %collective-permute-start.58 = (bf16[1,32,32,256]{3,2,1,0:T(8,128)(2,1)}, bf16[1,32,32,256]{3,2,1,0:T(8,128)(2,1)S(1)}, u32[]{:S(2)}, u32[]{:S(2)}) collective-permute-start(bf16[1,32,32,256]{3,2,1,0:T(8,128)(2,1)} %slice.446), channel_id=1, source_target_pairs={{0,18},{1,19},{2,16},{3,17},{4,22},{5,23},{6,20},{7,21},{8,26},{9,... | collective-permute-start | bytes 1572872 | tf_op jit(solution)/shard_map/ppermute | solution.py:164
  650.8 57.6 %collective-permute-start.57 = (bf16[1,32,32,256]{3,2,1,0:T(8,128)(2,1)}, bf16[1,32,32,256]{3,2,1,0:T(8,128)(2,1)S(1)}, u32[]{:S(2)}, u32[]{:S(2)}) collective-permute-start(bf16[1,32,32,256]{3,2,1,0:T(8,128)(2,1)} %slice.445), channel_id=1, source_target_pairs={{0,17},{1,16},{2,19},{3,18},{4,21},{5,20},{6,23},{7,22},{8,25},{9,... | collective-permute-start | bytes 1572872 | tf_op jit(solution)/shard_map/ppermute | solution.py:164
  652.2 56.9 %collective-permute-start.56 = (bf16[1,32,32,256]{3,2,1,0:T(8,128)(2,1)}, bf16[1,32,32,256]{3,2,1,0:T(8,128)(2,1)S(1)}, u32[]{:S(2)}, u32[]{:S(2)}) collective-permute-start(bf16[1,32,32,256]{3,2,1,0:T(8,128)(2,1)} %slice.444), channel_id=1, source_target_pairs={{0,16},{1,17},{2,18},{3,19},{4,20},{5,21},{6,22},{7,23},{8,24},{9,... | collective-permute-start | bytes 1572872 | tf_op jit(solution)/shard_map/ppermute | solution.py:164
  652.8 58.1 %collective-permute-start.55 = (bf16[1,32,32,256]{3,2,1,0:T(8,128)(2,1)}, bf16[1,32,32,256]{3,2,1,0:T(8,128)(2,1)S(1)}, u32[]{:S(2)}, u32[]{:S(2)}) collective-permute-start(bf16[1,32,32,256]{3,2,1,0:T(8,128)(2,1)} %slice.443), channel_id=1, source_target_pairs={{0,19},{1,18},{2,17},{3,16},{4,23},{5,22},{6,21},{7,20},{8,27},{9,... | collective-permute-start | bytes 1572872 | tf_op jit(solution)/shard_map/ppermute | solution.py:164
  653.8 58.0 %collective-permute-start.54 = (bf16[1,32,32,256]{3,2,1,0:T(8,128)(2,1)}, bf16[1,32,32,256]{3,2,1,0:T(8,128)(2,1)S(1)}, u32[]{:S(2)}, u32[]{:S(2)}) collective-permute-start(bf16[1,32,32,256]{3,2,1,0:T(8,128)(2,1)} %slice.442), channel_id=1, source_target_pairs={{0,18},{1,19},{2,16},{3,17},{4,22},{5,23},{6,20},{7,21},{8,26},{9,... | collective-permute-start | bytes 1572872 | tf_op jit(solution)/shard_map/ppermute | solution.py:164
  709.1 34.7 %collective-permute-start.51 = (bf16[1,32,32,256]{3,2,1,0:T(8,128)(2,1)S(1)}, bf16[1,32,32,256]{3,2,1,0:T(8,128)(2,1)S(1)}, u32[]{:S(2)}, u32[]{:S(2)}) collective-permute-start(bf16[1,32,32,256]{3,2,1,0:T(8,128)(2,1)S(1)} %slice.439), channel_id=1, source_target_pairs={{0,19},{1,18},{2,17},{3,16},{4,23},{5,22},{6,21},{7,20},{8,27},{9,... | collective-permute-start | bytes 1572872 | tf_op jit(solution)/shard_map/ppermute | solution.py:164
  710.9 68.7 %collective-permute-start.47 = (bf16[2,32,32,256]{3,2,1,0:T(8,128)(2,1)S(1)}, bf16[2,32,32,256]{3,2,1,0:T(8,128)(2,1)}, u32[]{:S(2)}, u32[]{:S(2)}) collective-permute-start(bf16[2,32,32,256]{3,2,1,0:T(8,128)(2,1)S(1)} %slice.435), channel_id=1, source_target_pairs={{0,3},{1,2},{2,1},{3,0},{4,7},{5,6},{6,5},{7,4},{8,11},{9,10},{10,... | collective-permute-start | bytes 3145736 | tf_op jit(solution)/shard_map/ppermute | solution.py:153
  711.9 70.6 %collective-permute-start.46 = (bf16[2,32,32,256]{3,2,1,0:T(8,128)(2,1)S(1)}, bf16[2,32,32,256]{3,2,1,0:T(8,128)(2,1)}, u32[]{:S(2)}, u32[]{:S(2)}) collective-permute-start(bf16[2,32,32,256]{3,2,1,0:T(8,128)(2,1)S(1)} %slice.433), channel_id=1, source_target_pairs={{0,2},{1,3},{2,0},{3,1},{4,6},{5,7},{6,4},{7,5},{8,10},{9,11},{10,... | collective-permute-start | bytes 3145736 | tf_op jit(solution)/shard_map/ppermute | solution.py:153
  721.1 35.4 %collective-permute-start.50 = (bf16[1,32,32,256]{3,2,1,0:T(8,128)(2,1)S(1)}, bf16[1,32,32,256]{3,2,1,0:T(8,128)(2,1)S(1)}, u32[]{:S(2)}, u32[]{:S(2)}) collective-permute-start(bf16[1,32,32,256]{3,2,1,0:T(8,128)(2,1)S(1)} %slice.438), channel_id=1, source_target_pairs={{0,18},{1,19},{2,16},{3,17},{4,22},{5,23},{6,20},{7,21},{8,26},{9,... | collective-permute-start | bytes 1572872 | tf_op jit(solution)/shard_map/ppermute | solution.py:164
  766.9 36.0 %collective-permute-start.35 = (bf16[2,32,32,256]{3,2,1,0:T(8,128)(2,1)}, bf16[2,32,32,256]{3,2,1,0:T(8,128)(2,1)}, u32[]{:S(2)}, u32[]{:S(2)}) collective-permute-start(bf16[2,32,32,256]{3,2,1,0:T(8,128)(2,1)} %slice.427), channel_id=1, source_target_pairs={{0,3},{1,2},{2,1},{3,0},{4,7},{5,6},{6,5},{7,4},{8,11},{9,10},{10,... | collective-permute-start | bytes 3145736 | tf_op jit(solution)/shard_map/ppermute | solution.py:153
  778.4 49.0 %collective-permute-start.34 = (bf16[2,32,32,256]{3,2,1,0:T(8,128)(2,1)}, bf16[2,32,32,256]{3,2,1,0:T(8,128)(2,1)}, u32[]{:S(2)}, u32[]{:S(2)}) collective-permute-start(bf16[2,32,32,256]{3,2,1,0:T(8,128)(2,1)} %slice.425), channel_id=1, source_target_pairs={{0,2},{1,3},{2,0},{3,1},{4,6},{5,7},{6,4},{7,5},{8,10},{9,11},{10,... | collective-permute-start | bytes 3145736 | tf_op jit(solution)/shard_map/ppermute | solution.py:153
  779.6 47.9 %collective-permute-start.33 = (bf16[2,32,32,256]{3,2,1,0:T(8,128)(2,1)}, bf16[2,32,32,256]{3,2,1,0:T(8,128)(2,1)}, u32[]{:S(2)}, u32[]{:S(2)}) collective-permute-start(bf16[2,32,32,256]{3,2,1,0:T(8,128)(2,1)} %slice.423), channel_id=1, source_target_pairs={{0,1},{1,0},{2,3},{3,2},{4,5},{5,4},{6,7},{7,6},{8,9},{9,8},{10,11... | collective-permute-start | bytes 3145736 | tf_op jit(solution)/shard_map/ppermute | solution.py:153
  782.5 65.3 %collective-permute-start.23 = (bf16[2,32,32,256]{3,2,1,0:T(8,128)(2,1)}, bf16[2,32,32,256]{3,2,1,0:T(8,128)(2,1)}, u32[]{:S(2)}, u32[]{:S(2)}) collective-permute-start(bf16[2,32,32,256]{3,2,1,0:T(8,128)(2,1)} %slice.419), channel_id=1, source_target_pairs={{0,3},{1,2},{2,1},{3,0},{4,7},{5,6},{6,5},{7,4},{8,11},{9,10},{10,... | collective-permute-start | bytes 3145736 | tf_op jit(solution)/shard_map/ppermute | solution.py:153
  790.6 81.8 %collective-permute-start.22 = (bf16[2,32,32,256]{3,2,1,0:T(8,128)(2,1)}, bf16[2,32,32,256]{3,2,1,0:T(8,128)(2,1)}, u32[]{:S(2)}, u32[]{:S(2)}) collective-permute-start(bf16[2,32,32,256]{3,2,1,0:T(8,128)(2,1)} %slice.417), channel_id=1, source_target_pairs={{0,2},{1,3},{2,0},{3,1},{4,6},{5,7},{6,4},{7,5},{8,10},{9,11},{10,... | collective-permute-start | bytes 3145736 | tf_op jit(solution)/shard_map/ppermute | solution.py:153
  802.9 69.5 %collective-permute-start.21 = (bf16[2,32,32,256]{3,2,1,0:T(8,128)(2,1)}, bf16[2,32,32,256]{3,2,1,0:T(8,128)(2,1)}, u32[]{:S(2)}, u32[]{:S(2)}) collective-permute-start(bf16[2,32,32,256]{3,2,1,0:T(8,128)(2,1)} %slice.415), channel_id=1, source_target_pairs={{0,1},{1,0},{2,3},{3,2},{4,5},{5,4},{6,7},{7,6},{8,9},{9,8},{10,11... | collective-permute-start | bytes 3145736 | tf_op jit(solution)/shard_map/ppermute | solution.py:153
  827.5 65.3 %collective-permute-start.11 = (bf16[2,32,32,256]{3,2,1,0:T(8,128)(2,1)}, bf16[2,32,32,256]{3,2,1,0:T(8,128)(2,1)S(1)}, u32[]{:S(2)}, u32[]{:S(2)}) collective-permute-start(bf16[2,32,32,256]{3,2,1,0:T(8,128)(2,1)} %slice.411), channel_id=1, source_target_pairs={{0,3},{1,2},{2,1},{3,0},{4,7},{5,6},{6,5},{7,4},{8,11},{9,10},{10,... | collective-permute-start | bytes 3145736 | tf_op jit(solution)/shard_map/ppermute | solution.py:153
  827.5 88.7 %collective-permute-start.10 = (bf16[2,32,32,256]{3,2,1,0:T(8,128)(2,1)}, bf16[2,32,32,256]{3,2,1,0:T(8,128)(2,1)S(1)}, u32[]{:S(2)}, u32[]{:S(2)}) collective-permute-start(bf16[2,32,32,256]{3,2,1,0:T(8,128)(2,1)} %slice.409), channel_id=1, source_target_pairs={{0,2},{1,3},{2,0},{3,1},{4,6},{5,7},{6,4},{7,5},{8,10},{9,11},{10,... | collective-permute-start | bytes 3145736 | tf_op jit(solution)/shard_map/ppermute | solution.py:153
  847.9 69.3 %collective-permute-start.9 = (bf16[2,32,32,256]{3,2,1,0:T(8,128)(2,1)}, bf16[2,32,32,256]{3,2,1,0:T(8,128)(2,1)S(1)}, u32[]{:S(2)}, u32[]{:S(2)}) collective-permute-start(bf16[2,32,32,256]{3,2,1,0:T(8,128)(2,1)} %slice.407), channel_id=1, source_target_pairs={{0,1},{1,0},{2,3},{3,2},{4,5},{5,4},{6,7},{7,6},{8,9},{9,8},{10,11... | collective-permute-start | bytes 3145736 | tf_op jit(solution)/shard_map/ppermute | solution.py:153
  (104 other events, 3098.8 us)

commit v2 on v1

--- a/solution.py
+++ b/solution.py
@@ -7,7 +7,7 @@
 from jax.experimental.pallas import tpu as pltpu
 from jax.sharding import PartitionSpec as P
 
-CHUNK_ROWS = 32
+CHUNK_ROWS = 16
 MIB = 1 << 20
 
 
@@ -16,6 +16,7 @@
     ups = refs[1 : outer]
     downs = refs[outer : 2 * outer - 1]
     first_ref, third_ref, out_ref = refs[2 * outer - 1 :]
+    made = out_ref.shape[2]
     place = lax.axis_index("mode") // (lax.axis_size("mode") // outer)
 
     def body(row, carry):
@@ -25,11 +26,14 @@
                 jnp.where(place >= hop, ups[hop - 1][row], downs[outer - hop - 1][row])
             )
         block = jnp.concatenate(blocks, axis=0) if len(blocks) > 1 else blocks[0]
+        mixed = jnp.dot(first_ref[...], block, preferred_element_type=jnp.float32)
+        high = mixed.astype(jnp.bfloat16)
+        low = (mixed - high.astype(jnp.float32)).astype(jnp.bfloat16)
         for term in range(terms):
-            inner = jnp.dot(block, third_ref[term], preferred_element_type=jnp.float32)
-            value = jnp.dot(
-                first_ref[term], inner.astype(jnp.bfloat16), preferred_element_type=jnp.float32
-            )
+            part = slice(term * made, (term + 1) * made)
+            matrix = third_ref[term]
+            value = jnp.dot(high[part], matrix, preferred_element_type=jnp.float32)
+            value += jnp.dot(low[part], matrix, preferred_element_type=jnp.float32)
             out_ref[term, row] = value.astype(jnp.bfloat16)
         return carry
 
@@ -43,11 +47,12 @@
     step_rows = min(rows, 8)
     piece = pl.BlockSpec((step_rows, held, depth), lambda i: (i, 0, 0))
     whole = lambda shape: pl.BlockSpec(shape, lambda i: (0,) * len(shape))
-    flops = 2 * terms * rows * depth * held * outer * (depth + made)
+    flops = 2 * terms * rows * depth * made * (held * outer + 2 * depth)
+    stacked = first.reshape(terms * made, first.shape[2])
     return pl.pallas_call(
         functools.partial(one_two_kernel, outer, terms, step_rows),
         grid=(rows // step_rows,),
-        in_specs=[piece] * (2 * outer - 1) + [whole(first.shape), whole(third.shape)],
+        in_specs=[piece] * (2 * outer - 1) + [whole(stacked.shape), whole(third.shape)],
         out_specs=pl.BlockSpec((terms, step_rows, made, depth), lambda i: (0, i, 0, 0)),
         out_shape=jax.ShapeDtypeStruct((terms, rows, made, depth), jnp.bfloat16),
         compiler_params=pltpu.CompilerParams(vmem_limit_bytes=48 * MIB),
@@ -57,7 +62,7 @@
             transcendentals=0,
         ),
         name="third_first",
-    )(own, *ups, *downs, first, third)
+    )(own, *ups, *downs, stacked, third)
 
 
 def final_kernel(pieces, *refs):
@@ -134,17 +139,10 @@
             for d in range(inner)
         ]
 
-    def ordered(matrix):
-        return [
-            block[:, start : start + chunk]
-            for start in range(0, share, chunk)
-            for block in columns(matrix)
-        ]
-
     second = []
     for term in range(terms - 1):
-        second += ordered(own_second[term])
-    second += ordered(other_second[terms - 1])
+        second += columns(own_second[term])
+    second += columns(other_second[terms - 1])
     second = jnp.concatenate(second, axis=1)
 
     turned = jnp.swapaxes(own_core, 0, 1)
@@ -179,11 +177,16 @@
                 pairs += [(z * inner + h, (z + way) * inner + h) for h in range(inner)]
         return lax.ppermute(value, "mode", pairs)
 
-    near, far = [], []
+    def after(*values):
+        mark = sum(value[0, 0, 0].astype(jnp.float32) for value in values)
+        return (mark * 0.0).astype(jnp.int32)
+
+    near, far, ready, older = [], [], 0, 0
     for start in range(0, share, chunk):
         pieces = []
         for d in range(inner):
-            piece = lax.dynamic_slice_in_dim(turned, partner(member, d) * share + start, chunk, 0)
+            row = partner(member, d) * share + start + ready
+            piece = lax.dynamic_slice_in_dim(turned, row, chunk, 0)
             pieces.append(exchange(piece, d) if d else piece)
         own = jnp.concatenate(pieces, axis=1)
         ups, downs = [], []
@@ -192,13 +195,16 @@
             up, down = relay(up, hop, 1), relay(down, hop, -1)
             ups.append(up)
             downs.append(down)
+        if ups:
+            ready, older = older, after(ups[1], downs[1])
         made = one_three(own, ups, downs, first, third)
         made = made.reshape(terms, chunk, inner, rows, depth)
         for d in range(inner):
             part = jnp.swapaxes(made[:, :, d], 1, 2)
             near.append(exchange(part[:-1], d) if d else part[:-1])
             far.append(crossed(part[-1:], d))
-    return final(near, far, second, own_core)[None]
+    by_member = lambda blocks: [block for d in range(inner) for block in blocks[d::inner]]
+    return final(by_member(near), by_member(far), second, own_core)[None]
 
 
 def solution(mesh):

time: 963 us -> 785 us (0.82)
  waiting for transfers between devices: 577 us -> 350 us
  starting transfers between devices: 78.6 us -> 159 us
  Pallas kernels: 175 us -> 120 us
  local copies, waits for them, and re-layouts: 110 us -> 129 us
  between operations: 1.39 us -> 11.6 us
    ppermute x24 -> x48, waiting for transfers between devices: 352 us -> 175 us  [relay(): return lax.ppermute(value, 'mode', pairs)]
    ppermute x24 -> x48, waiting for transfers between devices: 176 us -> 109 us  [exchange(): lax.ppermute(value, 'mode', [(z * inner + h, z * inner + partner(h, d)) f...]
    pallas_call x4 -> x8, Pallas kernels: 151 us -> 95.9 us  [one_three(): pl.pallas_call(functools.partial(one_two_kernel, outer, terms, step_rows)...]
    ppermute x24 -> x48, starting transfers between devices: 41.3 us -> 93.2 us  [relay(): return lax.ppermute(value, 'mode', pairs)]
    ppermute x16 -> x32, starting transfers between devices: 15.6 us -> 34.7 us  [crossed(): lax.ppermute(value, ('state', 'mode'), [(s * modes + z * inner + h, (stat...]
    ppermute x16 -> x32, waiting for transfers between devices: 49.6 us -> 65.8 us  [crossed(): lax.ppermute(value, ('state', 'mode'), [(s * modes + z * inner + h, (stat...]
    another operation x17 -> x36, local copies, waits for them, and re-layouts: 9.29 us -> 22.1 us
    ppermute x24 -> x48, starting transfers between devices: 21.8 us -> 31.3 us  [exchange(): lax.ppermute(value, 'mode', [(z * inner + h, z * inner + partner(h, d)) f...]
  transfers between devices with their start and end apart: 64 -> 128, of which waited for: 33 -> 51; matrix products, arithmetic and copies ran while one was open for 9% -> 14% of each run, Pallas kernels for 16% -> 12%
where the time goes in v2:
time: 785 us; the launch traced here: 777 us
  waiting for transfers between devices  350 us (45%)
  starting transfers between devices  159 us (20%)
  local copies, waits for them, and re-layouts  129 us (16%)
  Pallas kernels  120 us (15%)
  between operations  11.6 us (1%)
    ppermute x48, waiting for transfers between devices, relay(): return lax.ppermute(value, 'mode', pairs)  175 us
    ppermute x48, waiting for transfers between devices, exchange(): lax.ppermute(value, 'mode', [(z * inner + h, z * inner + partner(h, d)) f...  109 us
    pallas_call x8, Pallas kernels, one_three(): pl.pallas_call(functools.partial(one_two_kernel, outer, terms, step_rows)...  95.9 us
    ppermute x48, starting transfers between devices, relay(): return lax.ppermute(value, 'mode', pairs)  93.2 us
    ppermute x32, waiting for transfers between devices, crossed(): lax.ppermute(value, ('state', 'mode'), [(s * modes + z * inner + h, (stat...  65.8 us
    unnamed x395, local copies, waits for them, and re-layouts  50.8 us
    ppermute x32, starting transfers between devices, crossed(): lax.ppermute(value, ('state', 'mode'), [(s * modes + z * inner + h, (stat...  34.7 us
    ppermute x48, starting transfers between devices, exchange(): lax.ppermute(value, 'mode', [(z * inner + h, z * inner + partner(h, d)) f...  31.3 us
  transfers between devices with their start and end apart: 128, of which 51 were waited for; matrix products, arithmetic and copies ran while one was open for 14% of the time, Pallas kernels for 12%

profile of v2, /device:TPU:24, one launch (start us, length us, event | category | flops | bytes accessed | tf_op | source)
XLA Modules:
  0.0 776.8 jit_solution(3663186997830024955)
XLA Ops:
  6.6 4.6 collective-permute-done.10
  11.2 4.8 collective-permute-done.11
  22.5 4.8 collective-permute-done.2
  33.0 9.1 %collective-permute-done.15.refs_4_ = bf16[16,128,256]{2,1,0:T(8,128)(2,1)} collective-permute-done((bf16[16,128,256]{2,1,0:T(8,128)(2,1)S(1)}, bf16[16,128,256]{2,1,0:T(8,128)(2,1)}, u32[]{:S(2)}, u32[]{:S(2)}) %collective-permute-start.15) | collective-permute-done | bytes 1048608 | tf_op jit(solution)/shard_map/ppermute | solution.py:178
  48.7 15.4 %collective-permute-done.6.refs_4_ = bf16[16,128,256]{2,1,0:T(8,128)(2,1)} collective-permute-done((bf16[16,128,256]{2,1,0:T(8,128)(2,1)S(1)}, bf16[16,128,256]{2,1,0:T(8,128)(2,1)}, u32[]{:S(2)}, u32[]{:S(2)}) %collective-permute-start.6) | collective-permute-done | bytes 1048608 | tf_op jit(solution)/shard_map/ppermute | solution.py:178
  65.8 4.1 collective-permute-done.3.refs_1_
  72.5 19.9 %collective-permute-done.13.refs_2_ = bf16[16,128,256]{2,1,0:T(8,128)(2,1)} collective-permute-done((bf16[16,128,256]{2,1,0:T(8,128)(2,1)}, bf16[16,128,256]{2,1,0:T(8,128)(2,1)}, u32[]{:S(2)}, u32[]{:S(2)}) %collective-permute-start.13) | collective-permute-done | bytes 1048608 | tf_op jit(solution)/shard_map/ppermute | solution.py:178
  96.2 18.1 %collective-permute-done.4.refs_2_ = bf16[16,128,256]{2,1,0:T(8,128)(2,1)} collective-permute-done((bf16[16,128,256]{2,1,0:T(8,128)(2,1)}, bf16[16,128,256]{2,1,0:T(8,128)(2,1)}, u32[]{:S(2)}, u32[]{:S(2)}) %collective-permute-start.4) | collective-permute-done | bytes 1048608 | tf_op jit(solution)/shard_map/ppermute | solution.py:178
  143.3 4.4 collective-permute-done.29
  154.8 6.0 collective-permute-start.33
  163.2 4.6 collective-permute-start.24
  169.7 12.3 %third_first.9 = bf16[3,16,128,256]{3,2,1,0:T(8,128)(2,1)} custom-call(bf16[16,128,256]{2,1,0:T(8,128)(2,1)S(1)} %copy-done.5, bf16[16,128,256]{2,1,0:T(8,128)(2,1)} %collective-permute-done.12.refs_1_, bf16[16,128,256]{2,1,0:T(8,128)(2,1)} %collective-permute-done.13.refs_2_, bf16[16,128,256]{2,1,0:T(8,128)(2,1)} %collective-permute-done.14.refs_3_, ...), custom_call_target="tpu_custom_call" | custom-call | flops 3221225472 | bytes 10485760 | tf_op jit(solution)/shard_map/third_first/pallas_call | solution.py:52
  188.6 12.3 %third_first.8 = bf16[3,16,128,256]{3,2,1,0:T(8,128)(2,1)} custom-call(bf16[16,128,256]{2,1,0:T(8,128)(2,1)S(1)} %copy-done.3, bf16[16,128,256]{2,1,0:T(8,128)(2,1)} %collective-permute-done.3.refs_1_, bf16[16,128,256]{2,1,0:T(8,128)(2,1)} %collective-permute-done.4.refs_2_, bf16[16,128,256]{2,1,0:T(8,128)(2,1)} %collective-permute-done.5.refs_3_, ...), custom_call_target="tpu_custom_call" | custom-call | flops 3221225472 | bytes 10485760 | tf_op jit(solution)/shard_map/third_first/pallas_call | solution.py:52
  207.6 12.1 %collective-permute-done.21.refs_1_ = bf16[16,128,256]{2,1,0:T(8,128)(2,1)S(1)} collective-permute-done((bf16[16,128,256]{2,1,0:T(8,128)(2,1)S(1)}, bf16[16,128,256]{2,1,0:T(8,128)(2,1)S(1)}, u32[]{:S(2)}, u32[]{:S(2)}) %collective-permute-start.21) | collective-permute-done | bytes 1048608 | tf_op jit(solution)/shard_map/ppermute | solution.py:178
  230.1 6.1 collective-permute-done.112.refs_48_
  236.7 4.4 collective-permute-done.104.refs_40_
  241.9 5.2 collective-permute-done.96.refs_32_
  255.6 8.9 %collective-permute-done.81.refs_17_ = bf16[2,32,16,256]{3,2,1,0:T(8,128)(2,1)S(1)} collective-permute-done((bf16[2,32,16,256]{3,2,1,0:T(8,128)(2,1)S(1)}, bf16[2,32,16,256]{3,2,1,0:T(8,128)(2,1)S(1)}, u32[]{:S(2)}, u32[]{:S(2)}) %collective-permute-start.81) | collective-permute-done | bytes 524320 | tf_op jit(solution)/shard_map/ppermute | solution.py:151
  267.2 8.7 %collective-permute-done.22.refs_2_ = bf16[16,128,256]{2,1,0:T(8,128)(2,1)} collective-permute-done((bf16[16,128,256]{2,1,0:T(8,128)(2,1)S(1)}, bf16[16,128,256]{2,1,0:T(8,128)(2,1)}, u32[]{:S(2)}, u32[]{:S(2)}) %collective-permute-start.22) | collective-permute-done | bytes 1048608 | tf_op jit(solution)/shard_map/ppermute | solution.py:178
  297.5 12.0 %third_first.11 = bf16[3,16,128,256]{3,2,1,0:T(8,128)(2,1)} custom-call(bf16[16,128,256]{2,1,0:T(8,128)(2,1)S(1)} %pad_maximum_fusion.3.refs_0_, bf16[16,128,256]{2,1,0:T(8,128)(2,1)S(1)} %copy-done.91, bf16[16,128,256]{2,1,0:T(8,128)(2,1)} %collective-permute-done.31.refs_2_, bf16[16,128,256]{2,1,0:T(8,128)(2,1)} %collective-permute-done.32.refs_3_, ...), custom_call_target="tpu_custom_call" | custom-call | flops 3221225472 | bytes 10485760 | tf_op jit(solution)/shard_map/third_first/pallas_call | solution.py:52
  319.7 9.0 %collective-permute-done.47 = bf16[16,32,256]{2,1,0:T(8,128)(2,1)S(1)} collective-permute-done((bf16[16,32,256]{2,1,0:T(8,128)(2,1)S(1)}, bf16[16,32,256]{2,1,0:T(8,128)(2,1)S(1)}, u32[]{:S(2)}, u32[]{:S(2)}) %collective-permute-start.47) | collective-permute-done | bytes 262176 | tf_op jit(solution)/shard_map/ppermute | solution.py:151
  338.0 4.6 collective-permute-start.42
  345.4 11.8 %third_first.10 = bf16[3,16,128,256]{3,2,1,0:T(8,128)(2,1)} custom-call(bf16[16,128,256]{2,1,0:T(8,128)(2,1)S(1)} %pad_maximum_fusion.2.refs_0_, bf16[16,128,256]{2,1,0:T(8,128)(2,1)S(1)} %copy-done.81, bf16[16,128,256]{2,1,0:T(8,128)(2,1)} %collective-permute-done.22.refs_2_, bf16[16,128,256]{2,1,0:T(8,128)(2,1)S(1)} %collective-permute-done.23.refs_3_, ...), custom_call_target="tpu_custom_call" | custom-call | flops 3221225472 | bytes 10485760 | tf_op jit(solution)/shard_map/third_first/pallas_call | solution.py:52
  362.1 5.3 collective-permute-done.99.refs_35_
  369.0 7.8 %collective-permute-done.122.refs_58_ = bf16[1,32,16,256]{3,2,1,0:T(8,128)(2,1)S(1)} collective-permute-done((bf16[1,32,16,256]{3,2,1,0:T(8,128)(2,1)S(1)}, bf16[1,32,16,256]{3,2,1,0:T(8,128)(2,1)S(1)}, u32[]{:S(2)}, u32[]{:S(2)}) %collective-permute-start.122) | collective-permute-done | bytes 262176 | tf_op jit(solution)/shard_map/ppermute | solution.py:162
  378.8 7.2 collective-permute-done.114.refs_50_
  395.3 6.6 collective-permute-done.98.refs_34_
  403.3 12.6 %collective-permute-done.91.refs_27_ = bf16[2,32,16,256]{3,2,1,0:T(8,128)(2,1)S(1)} collective-permute-done((bf16[2,32,16,256]{3,2,1,0:T(8,128)(2,1)S(1)}, bf16[2,32,16,256]{3,2,1,0:T(8,128)(2,1)S(1)}, u32[]{:S(2)}, u32[]{:S(2)}) %collective-permute-start.91) | collective-permute-done | bytes 524320 | tf_op jit(solution)/shard_map/ppermute | solution.py:151
  422.9 17.2 %collective-permute-done.40.refs_2_ = bf16[16,128,256]{2,1,0:T(8,128)(2,1)} collective-permute-done((bf16[16,128,256]{2,1,0:T(8,128)(2,1)S(1)}, bf16[16,128,256]{2,1,0:T(8,128)(2,1)}, u32[]{:S(2)}, u32[]{:S(2)}) %collective-permute-start.40) | collective-permute-done | bytes 1048608 | tf_op jit(solution)/shard_map/ppermute | solution.py:178
  462.4 6.3 collective-permute-done.64
  468.9 5.4 collective-permute-done.55
  474.3 8.5 %collective-permute-start.69 = (bf16[16,128,256]{2,1,0:T(8,128)(2,1)S(1)}, bf16[16,128,256]{2,1,0:T(8,128)(2,1)S(1)}, u32[]{:S(2)}, u32[]{:S(2)}) collective-permute-start(bf16[16,128,256]{2,1,0:T(8,128)(2,1)S(1)} %pad_maximum_fusion.7.refs_0_), channel_id=1, source_target_pairs={{4,0},{5,1},{6,2},{7,3},{8,4},{9,5},{10,6},{11,7},{12,8},{13,9},{1... | collective-permute-start | bytes 3145736 | tf_op jit(solution)/shard_map/ppermute | solution.py:178
  485.6 5.2 collective-permute-start.60
  493.1 11.7 %third_first.13 = bf16[3,16,128,256]{3,2,1,0:T(8,128)(2,1)} custom-call(bf16[16,128,256]{2,1,0:T(8,128)(2,1)S(1)} %pad_maximum_fusion.5.refs_0_, bf16[16,128,256]{2,1,0:T(8,128)(2,1)S(1)} %copy-done.87, bf16[16,128,256]{2,1,0:T(8,128)(2,1)S(1)} %copy-done.93, bf16[16,128,256]{2,1,0:T(8,128)(2,1)S(1)} %collective-permute-done.50.refs_3_, ...), custom_call_target="tpu_custom_call" | custom-call | flops 3221225472 | bytes 10485760 | tf_op jit(solution)/shard_map/third_first/pallas_call | solution.py:52
  515.3 18.4 %collective-permute-done.41.refs_3_ = bf16[16,128,256]{2,1,0:T(8,128)(2,1)S(1)} collective-permute-done((bf16[16,128,256]{2,1,0:T(8,128)(2,1)}, bf16[16,128,256]{2,1,0:T(8,128)(2,1)S(1)}, u32[]{:S(2)}, u32[]{:S(2)}) %collective-permute-start.41) | collective-permute-done | bytes 1048608 | tf_op jit(solution)/shard_map/ppermute | solution.py:178
  535.6 20.5 %collective-permute-done.57.refs_1_ = bf16[16,128,256]{2,1,0:T(8,128)(2,1)S(1)} collective-permute-done((bf16[16,128,256]{2,1,0:T(8,128)(2,1)S(1)}, bf16[16,128,256]{2,1,0:T(8,128)(2,1)S(1)}, u32[]{:S(2)}, u32[]{:S(2)}) %collective-permute-start.57) | collective-permute-done | bytes 1048608 | tf_op jit(solution)/shard_map/ppermute | solution.py:178
  560.7 5.9 collective-permute-done.117.refs_53_
  566.6 11.9 %third_first.12 = bf16[3,16,128,256]{3,2,1,0:T(8,128)(2,1)} custom-call(bf16[16,128,256]{2,1,0:T(8,128)(2,1)S(1)} %pad_maximum_fusion.4.refs_0_, bf16[16,128,256]{2,1,0:T(8,128)(2,1)S(1)} %copy-done.83, bf16[16,128,256]{2,1,0:T(8,128)(2,1)} %collective-permute-done.40.refs_2_, bf16[16,128,256]{2,1,0:T(8,128)(2,1)S(1)} %collective-permute-done.41.refs_3_, ...), custom_call_target="tpu_custom_call" | custom-call | flops 3221225472 | bytes 10485760 | tf_op jit(solution)/shard_map/third_first/pallas_call | solution.py:52
  590.4 10.7 %collective-permute-done.58.refs_2_ = bf16[16,128,256]{2,1,0:T(8,128)(2,1)} collective-permute-done((bf16[16,128,256]{2,1,0:T(8,128)(2,1)S(1)}, bf16[16,128,256]{2,1,0:T(8,128)(2,1)}, u32[]{:S(2)}, u32[]{:S(2)}) %collective-permute-start.58) | collective-permute-done | bytes 1048608 | tf_op jit(solution)/shard_map/ppermute | solution.py:178
  619.5 4.1 collective-permute-done.68.refs_3_
  624.6 12.0 %third_first.15 = bf16[3,16,128,256]{3,2,1,0:T(8,128)(2,1)} custom-call(bf16[16,128,256]{2,1,0:T(8,128)(2,1)S(1)} %copy-done.7, bf16[16,128,256]{2,1,0:T(8,128)(2,1)S(1)} %copy-done.101, bf16[16,128,256]{2,1,0:T(8,128)(2,1)} %collective-permute-done.67.refs_2_, bf16[16,128,256]{2,1,0:T(8,128)(2,1)} %collective-permute-done.68.refs_3_, ...), custom_call_target="tpu_custom_call" | custom-call | flops 3221225472 | bytes 10485760 | tf_op jit(solution)/shard_map/third_first/pallas_call | solution.py:52
  640.1 5.5 collective-permute-done.59.refs_3_
  652.9 11.8 %third_first.14 = bf16[3,16,128,256]{3,2,1,0:T(8,128)(2,1)} custom-call(bf16[16,128,256]{2,1,0:T(8,128)(2,1)S(1)} %pad_maximum_fusion.6.refs_0_, bf16[16,128,256]{2,1,0:T(8,128)(2,1)S(1)} %copy-done.97, bf16[16,128,256]{2,1,0:T(8,128)(2,1)} %collective-permute-done.58.refs_2_, bf16[16,128,256]{2,1,0:T(8,128)(2,1)S(1)} %collective-permute-done.59.refs_3_, ...), custom_call_target="tpu_custom_call" | custom-call | flops 3221225472 | bytes 10485760 | tf_op jit(solution)/shard_map/third_first/pallas_call | solution.py:52
  668.4 16.8 %collective-permute-done.84.refs_20_ = bf16[2,32,16,256]{3,2,1,0:T(8,128)(2,1)S(1)} collective-permute-done((bf16[2,32,16,256]{3,2,1,0:T(8,128)(2,1)S(1)}, bf16[2,32,16,256]{3,2,1,0:T(8,128)(2,1)S(1)}, u32[]{:S(2)}, u32[]{:S(2)}) %collective-permute-start.84) | collective-permute-done | bytes 524320 | tf_op jit(solution)/shard_map/ppermute | solution.py:151
  711.7 4.5 collective-permute-done.110.refs_46_
  716.3 5.0 collective-permute-done.102.refs_38_
  735.2 11.6 %collective-permute-done.86.refs_22_ = bf16[2,32,16,256]{3,2,1,0:T(8,128)(2,1)S(1)} collective-permute-done((bf16[2,32,16,256]{3,2,1,0:T(8,128)(2,1)S(1)}, bf16[2,32,16,256]{3,2,1,0:T(8,128)(2,1)S(1)}, u32[]{:S(2)}, u32[]{:S(2)}) %collective-permute-start.86) | collective-permute-done | bytes 524320 | tf_op jit(solution)/shard_map/ppermute | solution.py:151
  751.9 24.4 %second_final.1 = f32[32,512,256]{2,1,0:T(8,128)} custom-call(bf16[2,32,16,256]{3,2,1,0:T(8,128)(2,1)S(1)} %slice.453.refs_0_, bf16[2,32,16,256]{3,2,1,0:T(8,128)(2,1)S(1)} %slice.455.refs_1_, bf16[2,32,16,256]{3,2,1,0:T(8,128)(2,1)S(1)} %slice.459.refs_2_, bf16[2,32,16,256]{3,2,1,0:T(8,128)(2,1)S(1)} %slice.463.refs_3_, ...), custom_call_target="tpu_custom_call" | custom-call | flops 12884901888 | bytes 50331648 | tf_op jit(solution)/shard_map/second_final/pallas_call | solution.py:86
  (746 shorter events, 304.8 us)
Async XLA Ops:
  27.4 36.8 %collective-permute-start.6 = (bf16[16,128,256]{2,1,0:T(8,128)(2,1)S(1)}, bf16[16,128,256]{2,1,0:T(8,128)(2,1)}, u32[]{:S(2)}, u32[]{:S(2)}) collective-permute-start(bf16[16,128,256]{2,1,0:T(8,128)(2,1)S(1)} %pad_maximum_fusion.refs_0_), channel_id=1, source_target_pairs={{4,0},{5,1},{6,2},{7,3},{8,4},{9,5},{10,6},{11,7},{12,8},{13,9},{1... | collective-permute-start | bytes 3145736 | tf_op jit(solution)/shard_map/ppermute | solution.py:178
  30.7 39.2 %collective-permute-start.3 = (bf16[16,128,256]{2,1,0:T(8,128)(2,1)S(1)}, bf16[16,128,256]{2,1,0:T(8,128)(2,1)}, u32[]{:S(2)}, u32[]{:S(2)}) collective-permute-start(bf16[16,128,256]{2,1,0:T(8,128)(2,1)S(1)} %pad_maximum_fusion.refs_0_), channel_id=1, source_target_pairs={{0,4},{1,5},{2,6},{3,7},{4,8},{5,9},{6,10},{7,11},{8,12},{9,13},{1... | collective-permute-start | bytes 3145736 | tf_op jit(solution)/shard_map/ppermute | solution.py:178
  47.4 44.9 %collective-permute-start.13 = (bf16[16,128,256]{2,1,0:T(8,128)(2,1)}, bf16[16,128,256]{2,1,0:T(8,128)(2,1)}, u32[]{:S(2)}, u32[]{:S(2)}) collective-permute-start(bf16[16,128,256]{2,1,0:T(8,128)(2,1)} %collective-permute-done.12.refs_1_), channel_id=1, source_target_pairs={{4,8},{5,9},{6,10},{7,11},{8,12},{9,13},{10,14},{11,15},{20,24},{2... | collective-permute-start | bytes 3145736 | tf_op jit(solution)/shard_map/ppermute | solution.py:178
  64.2 30.7 %collective-permute-start.7 = (bf16[16,128,256]{2,1,0:T(8,128)(2,1)}, bf16[16,128,256]{2,1,0:T(8,128)(2,1)}, u32[]{:S(2)}, u32[]{:S(2)}) collective-permute-start(bf16[16,128,256]{2,1,0:T(8,128)(2,1)} %collective-permute-done.6.refs_4_), channel_id=1, source_target_pairs={{4,0},{5,1},{6,2},{7,3},{8,4},{9,5},{10,6},{11,7},{20,16},{21,17},... | collective-permute-start | bytes 3145736 | tf_op jit(solution)/shard_map/ppermute | solution.py:178
  69.9 44.4 %collective-permute-start.4 = (bf16[16,128,256]{2,1,0:T(8,128)(2,1)}, bf16[16,128,256]{2,1,0:T(8,128)(2,1)}, u32[]{:S(2)}, u32[]{:S(2)}) collective-permute-start(bf16[16,128,256]{2,1,0:T(8,128)(2,1)} %collective-permute-done.3.refs_1_), channel_id=1, source_target_pairs={{4,8},{5,9},{6,10},{7,11},{8,12},{9,13},{10,14},{11,15},{20,24},{2... | collective-permute-start | bytes 3145736 | tf_op jit(solution)/shard_map/ppermute | solution.py:178
  120.9 39.9 %collective-permute-start.17 = (bf16[16,128,256]{2,1,0:T(8,128)(2,1)}, bf16[16,128,256]{2,1,0:T(8,128)(2,1)}, u32[]{:S(2)}, u32[]{:S(2)}) collective-permute-start(bf16[16,128,256]{2,1,0:T(8,128)(2,1)} %collective-permute-done.16.refs_5_), channel_id=1, source_target_pairs={{4,0},{5,1},{6,2},{7,3},{20,16},{21,17},{22,18},{23,19}} | collective-permute-start | bytes 3145736 | tf_op jit(solution)/shard_map/ppermute | solution.py:178
  125.9 37.4 %collective-permute-start.14 = (bf16[16,128,256]{2,1,0:T(8,128)(2,1)}, bf16[16,128,256]{2,1,0:T(8,128)(2,1)}, u32[]{:S(2)}, u32[]{:S(2)}) collective-permute-start(bf16[16,128,256]{2,1,0:T(8,128)(2,1)} %collective-permute-done.13.refs_2_), channel_id=1, source_target_pairs={{8,12},{9,13},{10,14},{11,15},{24,28},{25,29},{26,30},{27,31}} | collective-permute-start | bytes 3145736 | tf_op jit(solution)/shard_map/ppermute | solution.py:178
  127.9 40.0 %collective-permute-start.8 = (bf16[16,128,256]{2,1,0:T(8,128)(2,1)}, bf16[16,128,256]{2,1,0:T(8,128)(2,1)}, u32[]{:S(2)}, u32[]{:S(2)}) collective-permute-start(bf16[16,128,256]{2,1,0:T(8,128)(2,1)} %collective-permute-done.7.refs_5_), channel_id=1, source_target_pairs={{4,0},{5,1},{6,2},{7,3},{20,16},{21,17},{22,18},{23,19}} | collective-permute-start | bytes 3145736 | tf_op jit(solution)/shard_map/ppermute | solution.py:178
  147.6 38.7 %collective-permute-start.5 = (bf16[16,128,256]{2,1,0:T(8,128)(2,1)}, bf16[16,128,256]{2,1,0:T(8,128)(2,1)}, u32[]{:S(2)}, u32[]{:S(2)}) collective-permute-start(bf16[16,128,256]{2,1,0:T(8,128)(2,1)} %collective-permute-done.4.refs_2_), channel_id=1, source_target_pairs={{8,12},{9,13},{10,14},{11,15},{24,28},{25,29},{26,30},{27,31}} | collective-permute-start | bytes 3145736 | tf_op jit(solution)/shard_map/ppermute | solution.py:178
  154.8 46.1 %collective-permute-start.33 = (bf16[16,128,256]{2,1,0:T(8,128)(2,1)S(1)}, bf16[16,128,256]{2,1,0:T(8,128)(2,1)S(1)}, u32[]{:S(2)}, u32[]{:S(2)}) collective-permute-start(bf16[16,128,256]{2,1,0:T(8,128)(2,1)S(1)} %pad_maximum_fusion.3.refs_0_), channel_id=1, source_target_pairs={{4,0},{5,1},{6,2},{7,3},{8,4},{9,5},{10,6},{11,7},{12,8},{13,9},{1... | collective-permute-start | bytes 3145736 | tf_op jit(solution)/shard_map/ppermute | solution.py:178
  160.8 41.7 %collective-permute-start.30 = (bf16[16,128,256]{2,1,0:T(8,128)(2,1)S(1)}, bf16[16,128,256]{2,1,0:T(8,128)(2,1)S(1)}, u32[]{:S(2)}, u32[]{:S(2)}) collective-permute-start(bf16[16,128,256]{2,1,0:T(8,128)(2,1)S(1)} %pad_maximum_fusion.3.refs_0_), channel_id=1, source_target_pairs={{0,4},{1,5},{2,6},{3,7},{4,8},{5,9},{6,10},{7,11},{8,12},{9,13},{1... | collective-permute-start | bytes 3145736 | tf_op jit(solution)/shard_map/ppermute | solution.py:178
  163.2 42.8 %collective-permute-start.24 = (bf16[16,128,256]{2,1,0:T(8,128)(2,1)S(1)}, bf16[16,128,256]{2,1,0:T(8,128)(2,1)S(1)}, u32[]{:S(2)}, u32[]{:S(2)}) collective-permute-start(bf16[16,128,256]{2,1,0:T(8,128)(2,1)S(1)} %pad_maximum_fusion.2.refs_0_), channel_id=1, source_target_pairs={{4,0},{5,1},{6,2},{7,3},{8,4},{9,5},{10,6},{11,7},{12,8},{13,9},{1... | collective-permute-start | bytes 3145736 | tf_op jit(solution)/shard_map/ppermute | solution.py:178
  167.9 51.9 %collective-permute-start.21 = (bf16[16,128,256]{2,1,0:T(8,128)(2,1)S(1)}, bf16[16,128,256]{2,1,0:T(8,128)(2,1)S(1)}, u32[]{:S(2)}, u32[]{:S(2)}) collective-permute-start(bf16[16,128,256]{2,1,0:T(8,128)(2,1)S(1)} %pad_maximum_fusion.2.refs_0_), channel_id=1, source_target_pairs={{0,4},{1,5},{2,6},{3,7},{4,8},{5,9},{6,10},{7,11},{8,12},{9,13},{1... | collective-permute-start | bytes 3145736 | tf_op jit(solution)/shard_map/ppermute | solution.py:178
  186.4 37.0 %collective-permute-start.121 = (bf16[1,32,16,256]{3,2,1,0:T(8,128)(2,1)}, bf16[1,32,16,256]{3,2,1,0:T(8,128)(2,1)S(1)}, u32[]{:S(2)}, u32[]{:S(2)}) collective-permute-start(bf16[1,32,16,256]{3,2,1,0:T(8,128)(2,1)} %slice.553), channel_id=1, source_target_pairs={{0,19},{1,18},{2,17},{3,16},{4,23},{5,22},{6,21},{7,20},{8,27},{9,... | collective-permute-start | bytes 786440 | tf_op jit(solution)/shard_map/ppermute | solution.py:162
  251.5 43.6 %collective-permute-start.35 = (bf16[16,128,256]{2,1,0:T(8,128)(2,1)}, bf16[16,128,256]{2,1,0:T(8,128)(2,1)}, u32[]{:S(2)}, u32[]{:S(2)}) collective-permute-start(bf16[16,128,256]{2,1,0:T(8,128)(2,1)} %collective-permute-done.34.refs_5_), channel_id=1, source_target_pairs={{4,0},{5,1},{6,2},{7,3},{20,16},{21,17},{22,18},{23,19}} | collective-permute-start | bytes 3145736 | tf_op jit(solution)/shard_map/ppermute | solution.py:178
  253.4 44.1 %collective-permute-start.32 = (bf16[16,128,256]{2,1,0:T(8,128)(2,1)}, bf16[16,128,256]{2,1,0:T(8,128)(2,1)}, u32[]{:S(2)}, u32[]{:S(2)}) collective-permute-start(bf16[16,128,256]{2,1,0:T(8,128)(2,1)} %collective-permute-done.31.refs_2_), channel_id=1, source_target_pairs={{8,12},{9,13},{10,14},{11,15},{24,28},{25,29},{26,30},{27,31}} | collective-permute-start | bytes 3145736 | tf_op jit(solution)/shard_map/ppermute | solution.py:178
  288.6 48.1 %collective-permute-start.26 = (bf16[16,128,256]{2,1,0:T(8,128)(2,1)S(1)}, bf16[16,128,256]{2,1,0:T(8,128)(2,1)}, u32[]{:S(2)}, u32[]{:S(2)}) collective-permute-start(bf16[16,128,256]{2,1,0:T(8,128)(2,1)S(1)} %copy-done.171), channel_id=1, source_target_pairs={{4,0},{5,1},{6,2},{7,3},{20,16},{21,17},{22,18},{23,19}} | collective-permute-start | bytes 3145736 | tf_op jit(solution)/shard_map/ppermute | solution.py:178
  292.0 46.0 %collective-permute-start.23 = (bf16[16,128,256]{2,1,0:T(8,128)(2,1)}, bf16[16,128,256]{2,1,0:T(8,128)(2,1)S(1)}, u32[]{:S(2)}, u32[]{:S(2)}) collective-permute-start(bf16[16,128,256]{2,1,0:T(8,128)(2,1)} %collective-permute-done.22.refs_2_), channel_id=1, source_target_pairs={{8,12},{9,13},{10,14},{11,15},{24,28},{25,29},{26,30},{27,31}} | collective-permute-start | bytes 3145736 | tf_op jit(solution)/shard_map/ppermute | solution.py:178
  332.7 53.3 %collective-permute-start.51 = (bf16[16,128,256]{2,1,0:T(8,128)(2,1)S(1)}, bf16[16,128,256]{2,1,0:T(8,128)(2,1)S(1)}, u32[]{:S(2)}, u32[]{:S(2)}) collective-permute-start(bf16[16,128,256]{2,1,0:T(8,128)(2,1)S(1)} %pad_maximum_fusion.5.refs_0_), channel_id=1, source_target_pairs={{4,0},{5,1},{6,2},{7,3},{8,4},{9,5},{10,6},{11,7},{12,8},{13,9},{1... | collective-permute-start | bytes 3145736 | tf_op jit(solution)/shard_map/ppermute | solution.py:178
  336.7 50.1 %collective-permute-start.48 = (bf16[16,128,256]{2,1,0:T(8,128)(2,1)S(1)}, bf16[16,128,256]{2,1,0:T(8,128)(2,1)S(1)}, u32[]{:S(2)}, u32[]{:S(2)}) collective-permute-start(bf16[16,128,256]{2,1,0:T(8,128)(2,1)S(1)} %pad_maximum_fusion.5.refs_0_), channel_id=1, source_target_pairs={{0,4},{1,5},{2,6},{3,7},{4,8},{5,9},{6,10},{7,11},{8,12},{9,13},{1... | collective-permute-start | bytes 3145736 | tf_op jit(solution)/shard_map/ppermute | solution.py:178
  338.0 51.1 %collective-permute-start.42 = (bf16[16,128,256]{2,1,0:T(8,128)(2,1)S(1)}, bf16[16,128,256]{2,1,0:T(8,128)(2,1)S(1)}, u32[]{:S(2)}, u32[]{:S(2)}) collective-permute-start(bf16[16,128,256]{2,1,0:T(8,128)(2,1)S(1)} %pad_maximum_fusion.4.refs_0_), channel_id=1, source_target_pairs={{4,0},{5,1},{6,2},{7,3},{8,4},{9,5},{10,6},{11,7},{12,8},{13,9},{1... | collective-permute-start | bytes 3145736 | tf_op jit(solution)/shard_map/ppermute | solution.py:178
  343.3 46.5 %collective-permute-start.39 = (bf16[16,128,256]{2,1,0:T(8,128)(2,1)S(1)}, bf16[16,128,256]{2,1,0:T(8,128)(2,1)S(1)}, u32[]{:S(2)}, u32[]{:S(2)}) collective-permute-start(bf16[16,128,256]{2,1,0:T(8,128)(2,1)S(1)} %pad_maximum_fusion.4.refs_0_), channel_id=1, source_target_pairs={{0,4},{1,5},{2,6},{3,7},{4,8},{5,9},{6,10},{7,11},{8,12},{9,13},{1... | collective-permute-start | bytes 3145736 | tf_op jit(solution)/shard_map/ppermute | solution.py:178
  386.1 32.0 %collective-permute-start.52 = (bf16[16,128,256]{2,1,0:T(8,128)(2,1)S(1)}, bf16[16,128,256]{2,1,0:T(8,128)(2,1)S(1)}, u32[]{:S(2)}, u32[]{:S(2)}) collective-permute-start(bf16[16,128,256]{2,1,0:T(8,128)(2,1)S(1)} %collective-permute-done.51.refs_4_), channel_id=1, source_target_pairs={{4,0},{5,1},{6,2},{7,3},{8,4},{9,5},{10,6},{11,7},{20,16},{21,17},... | collective-permute-start | bytes 3145736 | tf_op jit(solution)/shard_map/ppermute | solution.py:178
  386.8 32.2 %collective-permute-start.49 = (bf16[16,128,256]{2,1,0:T(8,128)(2,1)S(1)}, bf16[16,128,256]{2,1,0:T(8,128)(2,1)S(1)}, u32[]{:S(2)}, u32[]{:S(2)}) collective-permute-start(bf16[16,128,256]{2,1,0:T(8,128)(2,1)S(1)} %collective-permute-done.48.refs_1_), channel_id=1, source_target_pairs={{4,8},{5,9},{6,10},{7,11},{8,12},{9,13},{10,14},{11,15},{20,24},{2... | collective-permute-start | bytes 3145736 | tf_op jit(solution)/shard_map/ppermute | solution.py:178
  389.1 32.4 %collective-permute-start.43 = (bf16[16,128,256]{2,1,0:T(8,128)(2,1)S(1)}, bf16[16,128,256]{2,1,0:T(8,128)(2,1)S(1)}, u32[]{:S(2)}, u32[]{:S(2)}) collective-permute-start(bf16[16,128,256]{2,1,0:T(8,128)(2,1)S(1)} %collective-permute-done.42.refs_4_), channel_id=1, source_target_pairs={{4,0},{5,1},{6,2},{7,3},{8,4},{9,5},{10,6},{11,7},{20,16},{21,17},... | collective-permute-start | bytes 3145736 | tf_op jit(solution)/shard_map/ppermute | solution.py:178
  389.8 50.3 %collective-permute-start.40 = (bf16[16,128,256]{2,1,0:T(8,128)(2,1)S(1)}, bf16[16,128,256]{2,1,0:T(8,128)(2,1)}, u32[]{:S(2)}, u32[]{:S(2)}) collective-permute-start(bf16[16,128,256]{2,1,0:T(8,128)(2,1)S(1)} %collective-permute-done.39.refs_1_), channel_id=1, source_target_pairs={{4,8},{5,9},{6,10},{7,11},{8,12},{9,13},{10,14},{11,15},{20,24},{2... | collective-permute-start | bytes 3145736 | tf_op jit(solution)/shard_map/ppermute | solution.py:178
  415.9 35.2 %collective-permute-start.83 = (bf16[2,32,16,256]{3,2,1,0:T(8,128)(2,1)}, bf16[2,32,16,256]{3,2,1,0:T(8,128)(2,1)}, u32[]{:S(2)}, u32[]{:S(2)}) collective-permute-start(bf16[2,32,16,256]{3,2,1,0:T(8,128)(2,1)} %slice.503), channel_id=1, source_target_pairs={{0,2},{1,3},{2,0},{3,1},{4,6},{5,7},{6,4},{7,5},{8,10},{9,11},{10,... | collective-permute-start | bytes 1572872 | tf_op jit(solution)/shard_map/ppermute | solution.py:151
  418.1 34.6 %collective-permute-start.75 = (bf16[2,32,16,256]{3,2,1,0:T(8,128)(2,1)}, bf16[2,32,16,256]{3,2,1,0:T(8,128)(2,1)}, u32[]{:S(2)}, u32[]{:S(2)}) collective-permute-start(bf16[2,32,16,256]{3,2,1,0:T(8,128)(2,1)} %slice.487), channel_id=1, source_target_pairs={{0,1},{1,0},{2,3},{3,2},{4,5},{5,4},{6,7},{7,6},{8,9},{9,8},{10,11... | collective-permute-start | bytes 1572872 | tf_op jit(solution)/shard_map/ppermute | solution.py:151
  419.0 33.9 %collective-permute-start.90 = (bf16[2,32,16,256]{3,2,1,0:T(8,128)(2,1)}, bf16[2,32,16,256]{3,2,1,0:T(8,128)(2,1)}, u32[]{:S(2)}, u32[]{:S(2)}) collective-permute-start(bf16[2,32,16,256]{3,2,1,0:T(8,128)(2,1)} %slice.517), channel_id=1, source_target_pairs={{0,3},{1,2},{2,1},{3,0},{4,7},{5,6},{6,5},{7,4},{8,11},{9,10},{10,... | collective-permute-start | bytes 1572872 | tf_op jit(solution)/shard_map/ppermute | solution.py:151
  421.4 32.1 %collective-permute-start.82 = (bf16[2,32,16,256]{3,2,1,0:T(8,128)(2,1)}, bf16[2,32,16,256]{3,2,1,0:T(8,128)(2,1)}, u32[]{:S(2)}, u32[]{:S(2)}) collective-permute-start(bf16[2,32,16,256]{3,2,1,0:T(8,128)(2,1)} %slice.501), channel_id=1, source_target_pairs={{0,2},{1,3},{2,0},{3,1},{4,6},{5,7},{6,4},{7,5},{8,10},{9,11},{10,... | collective-permute-start | bytes 1572872 | tf_op jit(solution)/shard_map/ppermute | solution.py:151
  452.9 31.3 %collective-permute-start.53 = (bf16[16,128,256]{2,1,0:T(8,128)(2,1)S(1)}, bf16[16,128,256]{2,1,0:T(8,128)(2,1)S(1)}, u32[]{:S(2)}, u32[]{:S(2)}) collective-permute-start(bf16[16,128,256]{2,1,0:T(8,128)(2,1)S(1)} %copy-done.173), channel_id=1, source_target_pairs={{4,0},{5,1},{6,2},{7,3},{20,16},{21,17},{22,18},{23,19}} | collective-permute-start | bytes 3145736 | tf_op jit(solution)/shard_map/ppermute | solution.py:178
  453.6 32.0 %collective-permute-start.50 = (bf16[16,128,256]{2,1,0:T(8,128)(2,1)S(1)}, bf16[16,128,256]{2,1,0:T(8,128)(2,1)S(1)}, u32[]{:S(2)}, u32[]{:S(2)}) collective-permute-start(bf16[16,128,256]{2,1,0:T(8,128)(2,1)S(1)} %copy-done.93), channel_id=1, source_target_pairs={{8,12},{9,13},{10,14},{11,15},{24,28},{25,29},{26,30},{27,31}} | collective-permute-start | bytes 3145736 | tf_op jit(solution)/shard_map/ppermute | solution.py:178
  455.1 35.7 %collective-permute-start.44 = (bf16[16,128,256]{2,1,0:T(8,128)(2,1)S(1)}, bf16[16,128,256]{2,1,0:T(8,128)(2,1)S(1)}, u32[]{:S(2)}, u32[]{:S(2)}) collective-permute-start(bf16[16,128,256]{2,1,0:T(8,128)(2,1)S(1)} %copy-done.169), channel_id=1, source_target_pairs={{4,0},{5,1},{6,2},{7,3},{20,16},{21,17},{22,18},{23,19}} | collective-permute-start | bytes 3145736 | tf_op jit(solution)/shard_map/ppermute | solution.py:178
  474.3 32.0 %collective-permute-start.69 = (bf16[16,128,256]{2,1,0:T(8,128)(2,1)S(1)}, bf16[16,128,256]{2,1,0:T(8,128)(2,1)S(1)}, u32[]{:S(2)}, u32[]{:S(2)}) collective-permute-start(bf16[16,128,256]{2,1,0:T(8,128)(2,1)S(1)} %pad_maximum_fusion.7.refs_0_), channel_id=1, source_target_pairs={{4,0},{5,1},{6,2},{7,3},{8,4},{9,5},{10,6},{11,7},{12,8},{13,9},{1... | collective-permute-start | bytes 3145736 | tf_op jit(solution)/shard_map/ppermute | solution.py:178
  484.2 49.5 %collective-permute-start.41 = (bf16[16,128,256]{2,1,0:T(8,128)(2,1)}, bf16[16,128,256]{2,1,0:T(8,128)(2,1)S(1)}, u32[]{:S(2)}, u32[]{:S(2)}) collective-permute-start(bf16[16,128,256]{2,1,0:T(8,128)(2,1)} %collective-permute-done.40.refs_2_), channel_id=1, source_target_pairs={{8,12},{9,13},{10,14},{11,15},{24,28},{25,29},{26,30},{27,31}} | collective-permute-start | bytes 3145736 | tf_op jit(solution)/shard_map/ppermute | solution.py:178
  485.6 48.3 %collective-permute-start.60 = (bf16[16,128,256]{2,1,0:T(8,128)(2,1)S(1)}, bf16[16,128,256]{2,1,0:T(8,128)(2,1)S(1)}, u32[]{:S(2)}, u32[]{:S(2)}) collective-permute-start(bf16[16,128,256]{2,1,0:T(8,128)(2,1)S(1)} %pad_maximum_fusion.6.refs_0_), channel_id=1, source_target_pairs={{4,0},{5,1},{6,2},{7,3},{8,4},{9,5},{10,6},{11,7},{12,8},{13,9},{1... | collective-permute-start | bytes 3145736 | tf_op jit(solution)/shard_map/ppermute | solution.py:178
  491.8 64.3 %collective-permute-start.57 = (bf16[16,128,256]{2,1,0:T(8,128)(2,1)S(1)}, bf16[16,128,256]{2,1,0:T(8,128)(2,1)S(1)}, u32[]{:S(2)}, u32[]{:S(2)}) collective-permute-start(bf16[16,128,256]{2,1,0:T(8,128)(2,1)S(1)} %pad_maximum_fusion.6.refs_0_), channel_id=1, source_target_pairs={{0,4},{1,5},{2,6},{3,7},{4,8},{5,9},{6,10},{7,11},{8,12},{9,13},{1... | collective-permute-start | bytes 3145736 | tf_op jit(solution)/shard_map/ppermute | solution.py:178
  506.3 73.5 %collective-permute-start.70 = (bf16[16,128,256]{2,1,0:T(8,128)(2,1)S(1)}, bf16[16,128,256]{2,1,0:T(8,128)(2,1)}, u32[]{:S(2)}, u32[]{:S(2)}) collective-permute-start(bf16[16,128,256]{2,1,0:T(8,128)(2,1)S(1)} %collective-permute-done.69.refs_4_), channel_id=1, source_target_pairs={{4,0},{5,1},{6,2},{7,3},{8,4},{9,5},{10,6},{11,7},{20,16},{21,17},... | collective-permute-start | bytes 3145736 | tf_op jit(solution)/shard_map/ppermute | solution.py:178
  511.2 70.2 %collective-permute-start.67 = (bf16[16,128,256]{2,1,0:T(8,128)(2,1)S(1)}, bf16[16,128,256]{2,1,0:T(8,128)(2,1)}, u32[]{:S(2)}, u32[]{:S(2)}) collective-permute-start(bf16[16,128,256]{2,1,0:T(8,128)(2,1)S(1)} %collective-permute-done.66.refs_1_), channel_id=1, source_target_pairs={{4,8},{5,9},{6,10},{7,11},{8,12},{9,13},{10,14},{11,15},{20,24},{2... | collective-permute-start | bytes 3145736 | tf_op jit(solution)/shard_map/ppermute | solution.py:178
  533.9 54.9 %collective-permute-start.61 = (bf16[16,128,256]{2,1,0:T(8,128)(2,1)S(1)}, bf16[16,128,256]{2,1,0:T(8,128)(2,1)}, u32[]{:S(2)}, u32[]{:S(2)}) collective-permute-start(bf16[16,128,256]{2,1,0:T(8,128)(2,1)S(1)} %collective-permute-done.60.refs_4_), channel_id=1, source_target_pairs={{4,0},{5,1},{6,2},{7,3},{8,4},{9,5},{10,6},{11,7},{20,16},{21,17},... | collective-permute-start | bytes 3145736 | tf_op jit(solution)/shard_map/ppermute | solution.py:178
  556.1 45.0 %collective-permute-start.58 = (bf16[16,128,256]{2,1,0:T(8,128)(2,1)S(1)}, bf16[16,128,256]{2,1,0:T(8,128)(2,1)}, u32[]{:S(2)}, u32[]{:S(2)}) collective-permute-start(bf16[16,128,256]{2,1,0:T(8,128)(2,1)S(1)} %collective-permute-done.57.refs_1_), channel_id=1, source_target_pairs={{4,8},{5,9},{6,10},{7,11},{8,12},{9,13},{10,14},{11,15},{20,24},{2... | collective-permute-start | bytes 3145736 | tf_op jit(solution)/shard_map/ppermute | solution.py:178
  579.8 38.3 %collective-permute-start.71 = (bf16[16,128,256]{2,1,0:T(8,128)(2,1)}, bf16[16,128,256]{2,1,0:T(8,128)(2,1)}, u32[]{:S(2)}, u32[]{:S(2)}) collective-permute-start(bf16[16,128,256]{2,1,0:T(8,128)(2,1)} %collective-permute-done.70.refs_5_), channel_id=1, source_target_pairs={{4,0},{5,1},{6,2},{7,3},{20,16},{21,17},{22,18},{23,19}} | collective-permute-start | bytes 3145736 | tf_op jit(solution)/shard_map/ppermute | solution.py:178
  581.4 42.2 %collective-permute-start.68 = (bf16[16,128,256]{2,1,0:T(8,128)(2,1)}, bf16[16,128,256]{2,1,0:T(8,128)(2,1)}, u32[]{:S(2)}, u32[]{:S(2)}) collective-permute-start(bf16[16,128,256]{2,1,0:T(8,128)(2,1)} %collective-permute-done.67.refs_2_), channel_id=1, source_target_pairs={{8,12},{9,13},{10,14},{11,15},{24,28},{25,29},{26,30},{27,31}} | collective-permute-start | bytes 3145736 | tf_op jit(solution)/shard_map/ppermute | solution.py:178
  588.8 50.1 %collective-permute-start.62 = (bf16[16,128,256]{2,1,0:T(8,128)(2,1)}, bf16[16,128,256]{2,1,0:T(8,128)(2,1)}, u32[]{:S(2)}, u32[]{:S(2)}) collective-permute-start(bf16[16,128,256]{2,1,0:T(8,128)(2,1)} %collective-permute-done.61.refs_5_), channel_id=1, source_target_pairs={{4,0},{5,1},{6,2},{7,3},{20,16},{21,17},{22,18},{23,19}} | collective-permute-start | bytes 3145736 | tf_op jit(solution)/shard_map/ppermute | solution.py:178
  601.2 44.5 %collective-permute-start.59 = (bf16[16,128,256]{2,1,0:T(8,128)(2,1)}, bf16[16,128,256]{2,1,0:T(8,128)(2,1)S(1)}, u32[]{:S(2)}, u32[]{:S(2)}) collective-permute-start(bf16[16,128,256]{2,1,0:T(8,128)(2,1)} %collective-permute-done.58.refs_2_), channel_id=1, source_target_pairs={{8,12},{9,13},{10,14},{11,15},{24,28},{25,29},{26,30},{27,31}} | collective-permute-start | bytes 3145736 | tf_op jit(solution)/shard_map/ppermute | solution.py:178
  638.9 46.4 %collective-permute-start.84 = (bf16[2,32,16,256]{3,2,1,0:T(8,128)(2,1)S(1)}, bf16[2,32,16,256]{3,2,1,0:T(8,128)(2,1)S(1)}, u32[]{:S(2)}, u32[]{:S(2)}) collective-permute-start(bf16[2,32,16,256]{3,2,1,0:T(8,128)(2,1)S(1)} %slice.505), channel_id=1, source_target_pairs={{0,2},{1,3},{2,0},{3,1},{4,6},{5,7},{6,4},{7,5},{8,10},{9,11},{10,... | collective-permute-start | bytes 1572872 | tf_op jit(solution)/shard_map/ppermute | solution.py:151
  645.7 39.6 %collective-permute-start.76 = (bf16[2,32,16,256]{3,2,1,0:T(8,128)(2,1)S(1)}, bf16[2,32,16,256]{3,2,1,0:T(8,128)(2,1)S(1)}, u32[]{:S(2)}, u32[]{:S(2)}) collective-permute-start(bf16[2,32,16,256]{3,2,1,0:T(8,128)(2,1)S(1)} %slice.489), channel_id=1, source_target_pairs={{0,1},{1,0},{2,3},{3,2},{4,5},{5,4},{6,7},{7,6},{8,9},{9,8},{10,11... | collective-permute-start | bytes 1572872 | tf_op jit(solution)/shard_map/ppermute | solution.py:151
  666.3 55.4 %collective-permute-start.95 = (bf16[2,32,16,256]{3,2,1,0:T(8,128)(2,1)}, bf16[2,32,16,256]{3,2,1,0:T(8,128)(2,1)S(1)}, u32[]{:S(2)}, u32[]{:S(2)}) collective-permute-start(bf16[2,32,16,256]{3,2,1,0:T(8,128)(2,1)} %slice.527), channel_id=1, source_target_pairs={{0,3},{1,2},{2,1},{3,0},{4,7},{5,6},{6,5},{7,4},{8,11},{9,10},{10,... | collective-permute-start | bytes 1572872 | tf_op jit(solution)/shard_map/ppermute | solution.py:151
  (256 other events, 3808.2 us)

commit v3 on v2

--- a/solution.py
+++ b/solution.py
@@ -7,7 +7,7 @@
 from jax.experimental.pallas import tpu as pltpu
 from jax.sharding import PartitionSpec as P
 
-CHUNK_ROWS = 16
+CHUNK_ROWS = 32
 MIB = 1 << 20
 
 

time: 785 us -> 777 us (0.990)
  waiting for transfers between devices: 350 us -> 479 us
  starting transfers between devices: 159 us -> 75.5 us
  local copies, waits for them, and re-layouts: 129 us -> 89.8 us
  Pallas kernels: 120 us -> 111 us
    ppermute x48 -> x24, waiting for transfers between devices: 175 us -> 274 us  [relay(): return lax.ppermute(value, 'mode', pairs)]
    ppermute x48 -> x24, starting transfers between devices: 93.2 us -> 45.4 us  [relay(): return lax.ppermute(value, 'mode', pairs)]
    ppermute x32 -> x16, starting transfers between devices: 34.7 us -> 14.5 us  [crossed(): lax.ppermute(value, ('state', 'mode'), [(s * modes + z * inner + h, (stat...]
    ppermute x32 -> x16, waiting for transfers between devices: 65.8 us -> 84.2 us  [crossed(): lax.ppermute(value, ('state', 'mode'), [(s * modes + z * inner + h, (stat...]
    ppermute x48 -> x24, starting transfers between devices: 31.3 us -> 15.6 us  [exchange(): lax.ppermute(value, 'mode', [(z * inner + h, z * inner + partner(h, d)) f...]
    ppermute x48 -> x24, waiting for transfers between devices: 109 us -> 121 us  [exchange(): lax.ppermute(value, 'mode', [(z * inner + h, z * inner + partner(h, d)) f...]
    slice x12 -> x4, local copies, waits for them, and re-layouts: 14.6 us -> 4.97 us  [after(): mark = sum((value[0, 0, 0].astype(jnp.float32) for value in values))]
    pallas_call x8 -> x4, Pallas kernels: 95.9 us -> 87.3 us  [one_three(): pl.pallas_call(functools.partial(one_two_kernel, outer, terms, step_rows)...]
  transfers between devices with their start and end apart: 128 -> 64, of which waited for: 51 -> 34; matrix products, arithmetic and copies ran while one was open for 14% -> 10% of each run, Pallas kernels for 12% -> 11%
where the time goes in v3:
time: 777 us; the launch traced here: 768 us
  waiting for transfers between devices  479 us (62%)
  Pallas kernels  111 us (14%)
  local copies, waits for them, and re-layouts  89.8 us (12%)
  starting transfers between devices  75.5 us (10%)
    ppermute x24, waiting for transfers between devices, relay(): return lax.ppermute(value, 'mode', pairs)  274 us
    ppermute x24, waiting for transfers between devices, exchange(): lax.ppermute(value, 'mode', [(z * inner + h, z * inner + partner(h, d)) f...  121 us
    pallas_call x4, Pallas kernels, one_three(): pl.pallas_call(functools.partial(one_two_kernel, outer, terms, step_rows)...  87.3 us
    ppermute x16, waiting for transfers between devices, crossed(): lax.ppermute(value, ('state', 'mode'), [(s * modes + z * inner + h, (stat...  84.2 us
    ppermute x24, starting transfers between devices, relay(): return lax.ppermute(value, 'mode', pairs)  45.4 us
    unnamed x149, local copies, waits for them, and re-layouts  42.4 us
    pallas_call x1, Pallas kernels, final(): pl.pallas_call(functools.partial(final_kernel, len(own)), grid=(rows // s...  24.2 us
    ppermute x24, starting transfers between devices, exchange(): lax.ppermute(value, 'mode', [(z * inner + h, z * inner + partner(h, d)) f...  15.6 us
  transfers between devices with their start and end apart: 64, of which 34 were waited for; matrix products, arithmetic and copies ran while one was open for 10% of the time, Pallas kernels for 11%

profile of v3, /device:TPU:24, one launch (start us, length us, event | category | flops | bytes accessed | tf_op | source)
XLA Modules:
  0.0 767.8 jit_solution(11957390730262140672)
XLA Ops:
  0.0 2.8 constant_dynamic-slice_fusion.11
  9.3 9.0 %collective-permute-done.10 = bf16[32,32,256]{2,1,0:T(8,128)(2,1)S(1)} collective-permute-done((bf16[32,32,256]{2,1,0:T(8,128)(2,1)S(1)}, bf16[32,32,256]{2,1,0:T(8,128)(2,1)S(1)}, u32[]{:S(2)}, u32[]{:S(2)}) %collective-permute-start.10) | collective-permute-done | bytes 524320 | tf_op jit(solution)/shard_map/ppermute | solution.py:151
  18.2 10.4 %collective-permute-done.11 = bf16[32,32,256]{2,1,0:T(8,128)(2,1)S(1)} collective-permute-done((bf16[32,32,256]{2,1,0:T(8,128)(2,1)S(1)}, bf16[32,32,256]{2,1,0:T(8,128)(2,1)S(1)}, u32[]{:S(2)}, u32[]{:S(2)}) %collective-permute-start.11) | collective-permute-done | bytes 524320 | tf_op jit(solution)/shard_map/ppermute | solution.py:151
  28.9 3.7 collective-permute-start.15
  33.8 6.9 collective-permute-done.1
  40.7 10.4 %collective-permute-done.2 = bf16[32,32,256]{2,1,0:T(8,128)(2,1)S(1)} collective-permute-done((bf16[32,32,256]{2,1,0:T(8,128)(2,1)S(1)}, bf16[32,32,256]{2,1,0:T(8,128)(2,1)S(1)}, u32[]{:S(2)}, u32[]{:S(2)}) %collective-permute-start.2) | collective-permute-done | bytes 524320 | tf_op jit(solution)/shard_map/ppermute | solution.py:151
  51.3 3.7 collective-permute-start.6
  57.6 19.6 %collective-permute-done.15.refs_4_ = bf16[32,128,256]{2,1,0:T(8,128)(2,1)} collective-permute-done((bf16[32,128,256]{2,1,0:T(8,128)(2,1)S(1)}, bf16[32,128,256]{2,1,0:T(8,128)(2,1)}, u32[]{:S(2)}, u32[]{:S(2)}) %collective-permute-start.15) | collective-permute-done | bytes 2097184 | tf_op jit(solution)/shard_map/ppermute | solution.py:178
  79.2 3.7 collective-permute-done.12.refs_1_
  84.2 37.6 %collective-permute-done.6.refs_4_ = bf16[32,128,256]{2,1,0:T(8,128)(2,1)} collective-permute-done((bf16[32,128,256]{2,1,0:T(8,128)(2,1)S(1)}, bf16[32,128,256]{2,1,0:T(8,128)(2,1)}, u32[]{:S(2)}, u32[]{:S(2)}) %collective-permute-start.6) | collective-permute-done | bytes 2097184 | tf_op jit(solution)/shard_map/ppermute | solution.py:178
  123.8 4.1 collective-permute-done.3.refs_1_
  130.4 42.4 %collective-permute-done.13.refs_2_ = bf16[32,128,256]{2,1,0:T(8,128)(2,1)} collective-permute-done((bf16[32,128,256]{2,1,0:T(8,128)(2,1)}, bf16[32,128,256]{2,1,0:T(8,128)(2,1)}, u32[]{:S(2)}, u32[]{:S(2)}) %collective-permute-start.13) | collective-permute-done | bytes 2097184 | tf_op jit(solution)/shard_map/ppermute | solution.py:178
  176.7 40.5 %collective-permute-done.4.refs_2_ = bf16[32,128,256]{2,1,0:T(8,128)(2,1)} collective-permute-done((bf16[32,128,256]{2,1,0:T(8,128)(2,1)}, bf16[32,128,256]{2,1,0:T(8,128)(2,1)}, u32[]{:S(2)}, u32[]{:S(2)}) %collective-permute-start.4) | collective-permute-done | bytes 2097184 | tf_op jit(solution)/shard_map/ppermute | solution.py:178
  219.9 6.2 constant_dynamic-slice_fusion.3
  234.3 6.3 collective-permute-done.29
  243.9 11.8 %collective-permute-done.28 = bf16[32,32,256]{2,1,0:T(8,128)(2,1)S(1)} collective-permute-done((bf16[32,32,256]{2,1,0:T(8,128)(2,1)S(1)}, bf16[32,32,256]{2,1,0:T(8,128)(2,1)S(1)}, u32[]{:S(2)}, u32[]{:S(2)}) %collective-permute-start.28) | collective-permute-done | bytes 524320 | tf_op jit(solution)/shard_map/ppermute | solution.py:151
  257.6 9.4 %collective-permute-done.19 = bf16[32,32,256]{2,1,0:T(8,128)(2,1)S(1)} collective-permute-done((bf16[32,32,256]{2,1,0:T(8,128)(2,1)S(1)}, bf16[32,32,256]{2,1,0:T(8,128)(2,1)S(1)}, u32[]{:S(2)}, u32[]{:S(2)}) %collective-permute-start.19) | collective-permute-done | bytes 524320 | tf_op jit(solution)/shard_map/ppermute | solution.py:151
  268.2 8.5 %collective-permute-done.20 = bf16[32,32,256]{2,1,0:T(8,128)(2,1)S(1)} collective-permute-done((bf16[32,32,256]{2,1,0:T(8,128)(2,1)S(1)}, bf16[32,32,256]{2,1,0:T(8,128)(2,1)S(1)}, u32[]{:S(2)}, u32[]{:S(2)}) %collective-permute-start.20) | collective-permute-done | bytes 524320 | tf_op jit(solution)/shard_map/ppermute | solution.py:151
  277.5 3.1 collective-permute-start.33
  284.7 3.0 pad_maximum_fusion.2.refs_0_
  289.0 5.9 collective-permute-start.24
  296.4 21.7 %third_first.5 = bf16[3,32,128,256]{3,2,1,0:T(8,128)(2,1)} custom-call(bf16[32,128,256]{2,1,0:T(8,128)(2,1)S(1)} %copy-done.5, bf16[32,128,256]{2,1,0:T(8,128)(2,1)} %collective-permute-done.12.refs_1_, bf16[32,128,256]{2,1,0:T(8,128)(2,1)} %collective-permute-done.13.refs_2_, bf16[32,128,256]{2,1,0:T(8,128)(2,1)} %collective-permute-done.14.refs_3_, ...), custom_call_target="tpu_custom_call" | custom-call | flops 6442450944 | bytes 20971520 | tf_op jit(solution)/shard_map/third_first/pallas_call | solution.py:52
  318.1 3.6 fusion.41
  323.5 2.5 collective-permute-done.5.refs_3_
  327.8 21.7 %third_first.4 = bf16[3,32,128,256]{3,2,1,0:T(8,128)(2,1)} custom-call(bf16[32,128,256]{2,1,0:T(8,128)(2,1)S(1)} %copy-done.3, bf16[32,128,256]{2,1,0:T(8,128)(2,1)} %collective-permute-done.3.refs_1_, bf16[32,128,256]{2,1,0:T(8,128)(2,1)} %collective-permute-done.4.refs_2_, bf16[32,128,256]{2,1,0:T(8,128)(2,1)} %collective-permute-done.5.refs_3_, ...), custom_call_target="tpu_custom_call" | custom-call | flops 6442450944 | bytes 20971520 | tf_op jit(solution)/shard_map/third_first/pallas_call | solution.py:52
  354.0 17.1 %collective-permute-done.30.refs_1_ = bf16[32,128,256]{2,1,0:T(8,128)(2,1)} collective-permute-done((bf16[32,128,256]{2,1,0:T(8,128)(2,1)}, bf16[32,128,256]{2,1,0:T(8,128)(2,1)}, u32[]{:S(2)}, u32[]{:S(2)}) %collective-permute-start.30) | collective-permute-done | bytes 2097184 | tf_op jit(solution)/shard_map/ppermute | solution.py:178
  371.9 43.2 %collective-permute-done.21.refs_1_ = bf16[32,128,256]{2,1,0:T(8,128)(2,1)} collective-permute-done((bf16[32,128,256]{2,1,0:T(8,128)(2,1)}, bf16[32,128,256]{2,1,0:T(8,128)(2,1)}, u32[]{:S(2)}, u32[]{:S(2)}) %collective-permute-start.21) | collective-permute-done | bytes 2097184 | tf_op jit(solution)/shard_map/ppermute | solution.py:178
  422.5 9.0 %collective-permute-done.49.refs_17_ = bf16[1,32,32,256]{3,2,1,0:T(8,128)(2,1)S(1)} collective-permute-done((bf16[1,32,32,256]{3,2,1,0:T(8,128)(2,1)S(1)}, bf16[1,32,32,256]{3,2,1,0:T(8,128)(2,1)S(1)}, u32[]{:S(2)}, u32[]{:S(2)}) %collective-permute-start.49) | collective-permute-done | bytes 524320 | tf_op jit(solution)/shard_map/ppermute | solution.py:162
  431.5 10.2 %collective-permute-done.60.refs_28_ = bf16[1,32,32,256]{3,2,1,0:T(8,128)(2,1)S(1)} collective-permute-done((bf16[1,32,32,256]{3,2,1,0:T(8,128)(2,1)S(1)}, bf16[1,32,32,256]{3,2,1,0:T(8,128)(2,1)S(1)}, u32[]{:S(2)}, u32[]{:S(2)}) %collective-permute-start.60) | collective-permute-done | bytes 524320 | tf_op jit(solution)/shard_map/ppermute | solution.py:162
  442.3 11.6 %collective-permute-done.56.refs_24_ = bf16[1,32,32,256]{3,2,1,0:T(8,128)(2,1)S(1)} collective-permute-done((bf16[1,32,32,256]{3,2,1,0:T(8,128)(2,1)S(1)}, bf16[1,32,32,256]{3,2,1,0:T(8,128)(2,1)S(1)}, u32[]{:S(2)}, u32[]{:S(2)}) %collective-permute-start.56) | collective-permute-done | bytes 524320 | tf_op jit(solution)/shard_map/ppermute | solution.py:162
  453.9 10.3 %collective-permute-done.52.refs_20_ = bf16[1,32,32,256]{3,2,1,0:T(8,128)(2,1)S(1)} collective-permute-done((bf16[1,32,32,256]{3,2,1,0:T(8,128)(2,1)S(1)}, bf16[1,32,32,256]{3,2,1,0:T(8,128)(2,1)S(1)}, u32[]{:S(2)}, u32[]{:S(2)}) %collective-permute-start.52) | collective-permute-done | bytes 524320 | tf_op jit(solution)/shard_map/ppermute | solution.py:162
  466.2 8.4 %collective-permute-done.48.refs_16_ = bf16[1,32,32,256]{3,2,1,0:T(8,128)(2,1)S(1)} collective-permute-done((bf16[1,32,32,256]{3,2,1,0:T(8,128)(2,1)S(1)}, bf16[1,32,32,256]{3,2,1,0:T(8,128)(2,1)S(1)}, u32[]{:S(2)}, u32[]{:S(2)}) %collective-permute-start.48) | collective-permute-done | bytes 524320 | tf_op jit(solution)/shard_map/ppermute | solution.py:162
  476.0 3.3 collective-permute-done.45.refs_13_
  482.2 22.3 %collective-permute-done.41.refs_9_ = bf16[2,32,32,256]{3,2,1,0:T(8,128)(2,1)S(1)} collective-permute-done((bf16[2,32,32,256]{3,2,1,0:T(8,128)(2,1)S(1)}, bf16[2,32,32,256]{3,2,1,0:T(8,128)(2,1)S(1)}, u32[]{:S(2)}, u32[]{:S(2)}) %collective-permute-start.41) | collective-permute-done | bytes 1048608 | tf_op jit(solution)/shard_map/ppermute | solution.py:151
  506.4 19.2 %collective-permute-done.22.refs_2_ = bf16[32,128,256]{2,1,0:T(8,128)(2,1)} collective-permute-done((bf16[32,128,256]{2,1,0:T(8,128)(2,1)}, bf16[32,128,256]{2,1,0:T(8,128)(2,1)}, u32[]{:S(2)}, u32[]{:S(2)}) %collective-permute-start.22) | collective-permute-done | bytes 2097184 | tf_op jit(solution)/shard_map/ppermute | solution.py:178
  531.2 39.4 %collective-permute-done.32.refs_3_ = bf16[32,128,256]{2,1,0:T(8,128)(2,1)S(1)} collective-permute-done((bf16[32,128,256]{2,1,0:T(8,128)(2,1)S(1)}, bf16[32,128,256]{2,1,0:T(8,128)(2,1)S(1)}, u32[]{:S(2)}, u32[]{:S(2)}) %collective-permute-start.32) | collective-permute-done | bytes 2097184 | tf_op jit(solution)/shard_map/ppermute | solution.py:178
  571.8 21.9 %third_first.7 = bf16[3,32,128,256]{3,2,1,0:T(8,128)(2,1)} custom-call(bf16[32,128,256]{2,1,0:T(8,128)(2,1)} %pad_maximum_fusion.3.refs_0_, bf16[32,128,256]{2,1,0:T(8,128)(2,1)} %collective-permute-done.30.refs_1_, bf16[32,128,256]{2,1,0:T(8,128)(2,1)} %copy-done.58, bf16[32,128,256]{2,1,0:T(8,128)(2,1)} %copy-done.60, ...), custom_call_target="tpu_custom_call" | custom-call | flops 6442450944 | bytes 20971520 | tf_op jit(solution)/shard_map/third_first/pallas_call | solution.py:52
  593.7 3.6 fusion.39
  608.3 4.5 collective-permute-done.23.refs_3_
  614.3 22.1 %third_first.6 = bf16[3,32,128,256]{3,2,1,0:T(8,128)(2,1)} custom-call(bf16[32,128,256]{2,1,0:T(8,128)(2,1)} %pad_maximum_fusion.2.refs_0_, bf16[32,128,256]{2,1,0:T(8,128)(2,1)} %collective-permute-done.21.refs_1_, bf16[32,128,256]{2,1,0:T(8,128)(2,1)} %collective-permute-done.22.refs_2_, bf16[32,128,256]{2,1,0:T(8,128)(2,1)} %collective-permute-done.23.refs_3_, ...), custom_call_target="tpu_custom_call" | custom-call | flops 6442450944 | bytes 20971520 | tf_op jit(solution)/shard_map/third_first/pallas_call | solution.py:52
  636.4 3.6 fusion.40
  646.7 5.9 collective-permute-done.51.refs_19_
  665.2 10.9 %collective-permute-done.58.refs_26_ = bf16[1,32,32,256]{3,2,1,0:T(8,128)(2,1)S(1)} collective-permute-done((bf16[1,32,32,256]{3,2,1,0:T(8,128)(2,1)S(1)}, bf16[1,32,32,256]{3,2,1,0:T(8,128)(2,1)S(1)}, u32[]{:S(2)}, u32[]{:S(2)}) %collective-permute-start.58) | collective-permute-done | bytes 524320 | tf_op jit(solution)/shard_map/ppermute | solution.py:162
  676.9 8.5 %collective-permute-done.54.refs_22_ = bf16[1,32,32,256]{3,2,1,0:T(8,128)(2,1)S(1)} collective-permute-done((bf16[1,32,32,256]{3,2,1,0:T(8,128)(2,1)S(1)}, bf16[1,32,32,256]{3,2,1,0:T(8,128)(2,1)S(1)}, u32[]{:S(2)}, u32[]{:S(2)}) %collective-permute-start.54) | collective-permute-done | bytes 524320 | tf_op jit(solution)/shard_map/ppermute | solution.py:162
  686.2 2.3 collective-permute-start.46
  688.5 8.5 %collective-permute-done.50.refs_18_ = bf16[1,32,32,256]{3,2,1,0:T(8,128)(2,1)S(1)} collective-permute-done((bf16[1,32,32,256]{3,2,1,0:T(8,128)(2,1)S(1)}, bf16[1,32,32,256]{3,2,1,0:T(8,128)(2,1)S(1)}, u32[]{:S(2)}, u32[]{:S(2)}) %collective-permute-start.50) | collective-permute-done | bytes 524320 | tf_op jit(solution)/shard_map/ppermute | solution.py:162
  720.5 22.5 %collective-permute-done.42.refs_10_ = bf16[2,32,32,256]{3,2,1,0:T(8,128)(2,1)} collective-permute-done((bf16[2,32,32,256]{3,2,1,0:T(8,128)(2,1)}, bf16[2,32,32,256]{3,2,1,0:T(8,128)(2,1)}, u32[]{:S(2)}, u32[]{:S(2)}) %collective-permute-start.42) | collective-permute-done | bytes 1048608 | tf_op jit(solution)/shard_map/ppermute | solution.py:151
  743.1 24.2 %second_final.1 = f32[32,512,256]{2,1,0:T(8,128)} custom-call(bf16[2,32,32,256]{3,2,1,0:T(8,128)(2,1)S(1)} %slice.229.refs_0_, bf16[2,32,32,256]{3,2,1,0:T(8,128)(2,1)S(1)} %slice.231.refs_1_, bf16[2,32,32,256]{3,2,1,0:T(8,128)(2,1)S(1)} %slice.235.refs_2_, bf16[2,32,32,256]{3,2,1,0:T(8,128)(2,1)S(1)} %slice.239.refs_3_, ...), custom_call_target="tpu_custom_call" | custom-call | flops 12884901888 | bytes 50331648 | tf_op jit(solution)/shard_map/second_final/pallas_call | solution.py:86
  (302 shorter events, 132.7 us)
Async XLA Ops:
  6.7 34.0 %collective-permute-start.1 = (bf16[32,32,256]{2,1,0:T(8,128)(2,1)S(1)}, bf16[32,32,256]{2,1,0:T(8,128)(2,1)S(1)}, u32[]{:S(2)}, u32[]{:S(2)}) collective-permute-start(bf16[32,32,256]{2,1,0:T(8,128)(2,1)S(1)} %bitcast.288), channel_id=1, source_target_pairs={{0,2},{1,3},{2,0},{3,1},{4,6},{5,7},{6,4},{7,5},{8,10},{9,11},{10,... | collective-permute-start | bytes 1572872 | tf_op jit(solution)/shard_map/ppermute | solution.py:151
  8.6 42.6 %collective-permute-start.2 = (bf16[32,32,256]{2,1,0:T(8,128)(2,1)S(1)}, bf16[32,32,256]{2,1,0:T(8,128)(2,1)S(1)}, u32[]{:S(2)}, u32[]{:S(2)}) collective-permute-start(bf16[32,32,256]{2,1,0:T(8,128)(2,1)S(1)} %bitcast.289), channel_id=1, source_target_pairs={{0,3},{1,2},{2,1},{3,0},{4,7},{5,6},{6,5},{7,4},{8,11},{9,10},{10,... | collective-permute-start | bytes 1572872 | tf_op jit(solution)/shard_map/ppermute | solution.py:151
  28.9 48.4 %collective-permute-start.15 = (bf16[32,128,256]{2,1,0:T(8,128)(2,1)S(1)}, bf16[32,128,256]{2,1,0:T(8,128)(2,1)}, u32[]{:S(2)}, u32[]{:S(2)}) collective-permute-start(bf16[32,128,256]{2,1,0:T(8,128)(2,1)S(1)} %pad_maximum_fusion.1.refs_0_), channel_id=1, source_target_pairs={{4,0},{5,1},{6,2},{7,3},{8,4},{9,5},{10,6},{11,7},{12,8},{13,9},{1... | collective-permute-start | bytes 6291464 | tf_op jit(solution)/shard_map/ppermute | solution.py:178
  32.5 50.4 %collective-permute-start.12 = (bf16[32,128,256]{2,1,0:T(8,128)(2,1)S(1)}, bf16[32,128,256]{2,1,0:T(8,128)(2,1)}, u32[]{:S(2)}, u32[]{:S(2)}) collective-permute-start(bf16[32,128,256]{2,1,0:T(8,128)(2,1)S(1)} %pad_maximum_fusion.1.refs_0_), channel_id=1, source_target_pairs={{0,4},{1,5},{2,6},{3,7},{4,8},{5,9},{6,10},{7,11},{8,12},{9,13},{1... | collective-permute-start | bytes 6291464 | tf_op jit(solution)/shard_map/ppermute | solution.py:178
  51.3 70.5 %collective-permute-start.6 = (bf16[32,128,256]{2,1,0:T(8,128)(2,1)S(1)}, bf16[32,128,256]{2,1,0:T(8,128)(2,1)}, u32[]{:S(2)}, u32[]{:S(2)}) collective-permute-start(bf16[32,128,256]{2,1,0:T(8,128)(2,1)S(1)} %pad_maximum_fusion.refs_0_), channel_id=1, source_target_pairs={{4,0},{5,1},{6,2},{7,3},{8,4},{9,5},{10,6},{11,7},{12,8},{13,9},{1... | collective-permute-start | bytes 6291464 | tf_op jit(solution)/shard_map/ppermute | solution.py:178
  55.0 72.9 %collective-permute-start.3 = (bf16[32,128,256]{2,1,0:T(8,128)(2,1)S(1)}, bf16[32,128,256]{2,1,0:T(8,128)(2,1)}, u32[]{:S(2)}, u32[]{:S(2)}) collective-permute-start(bf16[32,128,256]{2,1,0:T(8,128)(2,1)S(1)} %pad_maximum_fusion.refs_0_), channel_id=1, source_target_pairs={{0,4},{1,5},{2,6},{3,7},{4,8},{5,9},{6,10},{7,11},{8,12},{9,13},{1... | collective-permute-start | bytes 6291464 | tf_op jit(solution)/shard_map/ppermute | solution.py:178
  77.2 52.0 %collective-permute-start.16 = (bf16[32,128,256]{2,1,0:T(8,128)(2,1)}, bf16[32,128,256]{2,1,0:T(8,128)(2,1)}, u32[]{:S(2)}, u32[]{:S(2)}) collective-permute-start(bf16[32,128,256]{2,1,0:T(8,128)(2,1)} %collective-permute-done.15.refs_4_), channel_id=1, source_target_pairs={{4,0},{5,1},{6,2},{7,3},{8,4},{9,5},{10,6},{11,7},{20,16},{21,17},... | collective-permute-start | bytes 6291464 | tf_op jit(solution)/shard_map/ppermute | solution.py:178
  83.0 89.9 %collective-permute-start.13 = (bf16[32,128,256]{2,1,0:T(8,128)(2,1)}, bf16[32,128,256]{2,1,0:T(8,128)(2,1)}, u32[]{:S(2)}, u32[]{:S(2)}) collective-permute-start(bf16[32,128,256]{2,1,0:T(8,128)(2,1)} %collective-permute-done.12.refs_1_), channel_id=1, source_target_pairs={{4,8},{5,9},{6,10},{7,11},{8,12},{9,13},{10,14},{11,15},{20,24},{2... | collective-permute-start | bytes 6291464 | tf_op jit(solution)/shard_map/ppermute | solution.py:178
  121.8 53.7 %collective-permute-start.7 = (bf16[32,128,256]{2,1,0:T(8,128)(2,1)}, bf16[32,128,256]{2,1,0:T(8,128)(2,1)}, u32[]{:S(2)}, u32[]{:S(2)}) collective-permute-start(bf16[32,128,256]{2,1,0:T(8,128)(2,1)} %collective-permute-done.6.refs_4_), channel_id=1, source_target_pairs={{4,0},{5,1},{6,2},{7,3},{8,4},{9,5},{10,6},{11,7},{20,16},{21,17},... | collective-permute-start | bytes 6291464 | tf_op jit(solution)/shard_map/ppermute | solution.py:178
  127.9 89.3 %collective-permute-start.4 = (bf16[32,128,256]{2,1,0:T(8,128)(2,1)}, bf16[32,128,256]{2,1,0:T(8,128)(2,1)}, u32[]{:S(2)}, u32[]{:S(2)}) collective-permute-start(bf16[32,128,256]{2,1,0:T(8,128)(2,1)} %collective-permute-done.3.refs_1_), channel_id=1, source_target_pairs={{4,8},{5,9},{6,10},{7,11},{8,12},{9,13},{10,14},{11,15},{20,24},{2... | collective-permute-start | bytes 6291464 | tf_op jit(solution)/shard_map/ppermute | solution.py:178
  228.5 59.2 %collective-permute-start.17 = (bf16[32,128,256]{2,1,0:T(8,128)(2,1)}, bf16[32,128,256]{2,1,0:T(8,128)(2,1)}, u32[]{:S(2)}, u32[]{:S(2)}) collective-permute-start(bf16[32,128,256]{2,1,0:T(8,128)(2,1)} %collective-permute-done.16.refs_5_), channel_id=1, source_target_pairs={{4,0},{5,1},{6,2},{7,3},{20,16},{21,17},{22,18},{23,19}} | collective-permute-start | bytes 6291464 | tf_op jit(solution)/shard_map/ppermute | solution.py:178
  230.5 58.5 %collective-permute-start.14 = (bf16[32,128,256]{2,1,0:T(8,128)(2,1)}, bf16[32,128,256]{2,1,0:T(8,128)(2,1)}, u32[]{:S(2)}, u32[]{:S(2)}) collective-permute-start(bf16[32,128,256]{2,1,0:T(8,128)(2,1)} %collective-permute-done.13.refs_2_), channel_id=1, source_target_pairs={{8,12},{9,13},{10,14},{11,15},{24,28},{25,29},{26,30},{27,31}} | collective-permute-start | bytes 6291464 | tf_op jit(solution)/shard_map/ppermute | solution.py:178
  231.7 63.1 %collective-permute-start.8 = (bf16[32,128,256]{2,1,0:T(8,128)(2,1)}, bf16[32,128,256]{2,1,0:T(8,128)(2,1)}, u32[]{:S(2)}, u32[]{:S(2)}) collective-permute-start(bf16[32,128,256]{2,1,0:T(8,128)(2,1)} %collective-permute-done.7.refs_5_), channel_id=1, source_target_pairs={{4,0},{5,1},{6,2},{7,3},{20,16},{21,17},{22,18},{23,19}} | collective-permute-start | bytes 6291464 | tf_op jit(solution)/shard_map/ppermute | solution.py:178
  266.9 59.2 %collective-permute-start.5 = (bf16[32,128,256]{2,1,0:T(8,128)(2,1)}, bf16[32,128,256]{2,1,0:T(8,128)(2,1)}, u32[]{:S(2)}, u32[]{:S(2)}) collective-permute-start(bf16[32,128,256]{2,1,0:T(8,128)(2,1)} %collective-permute-done.4.refs_2_), channel_id=1, source_target_pairs={{8,12},{9,13},{10,14},{11,15},{24,28},{25,29},{26,30},{27,31}} | collective-permute-start | bytes 6291464 | tf_op jit(solution)/shard_map/ppermute | solution.py:178
  277.5 48.6 %collective-permute-start.33 = (bf16[32,128,256]{2,1,0:T(8,128)(2,1)}, bf16[32,128,256]{2,1,0:T(8,128)(2,1)}, u32[]{:S(2)}, u32[]{:S(2)}) collective-permute-start(bf16[32,128,256]{2,1,0:T(8,128)(2,1)} %pad_maximum_fusion.3.refs_0_), channel_id=1, source_target_pairs={{4,0},{5,1},{6,2},{7,3},{8,4},{9,5},{10,6},{11,7},{12,8},{13,9},{1... | collective-permute-start | bytes 6291464 | tf_op jit(solution)/shard_map/ppermute | solution.py:178
  287.7 83.4 %collective-permute-start.30 = (bf16[32,128,256]{2,1,0:T(8,128)(2,1)}, bf16[32,128,256]{2,1,0:T(8,128)(2,1)}, u32[]{:S(2)}, u32[]{:S(2)}) collective-permute-start(bf16[32,128,256]{2,1,0:T(8,128)(2,1)} %pad_maximum_fusion.3.refs_0_), channel_id=1, source_target_pairs={{0,4},{1,5},{2,6},{3,7},{4,8},{5,9},{6,10},{7,11},{8,12},{9,13},{1... | collective-permute-start | bytes 6291464 | tf_op jit(solution)/shard_map/ppermute | solution.py:178
  289.0 82.1 %collective-permute-start.24 = (bf16[32,128,256]{2,1,0:T(8,128)(2,1)}, bf16[32,128,256]{2,1,0:T(8,128)(2,1)}, u32[]{:S(2)}, u32[]{:S(2)}) collective-permute-start(bf16[32,128,256]{2,1,0:T(8,128)(2,1)} %pad_maximum_fusion.2.refs_0_), channel_id=1, source_target_pairs={{4,0},{5,1},{6,2},{7,3},{8,4},{9,5},{10,6},{11,7},{12,8},{13,9},{1... | collective-permute-start | bytes 6291464 | tf_op jit(solution)/shard_map/ppermute | solution.py:178
  294.9 120.2 %collective-permute-start.21 = (bf16[32,128,256]{2,1,0:T(8,128)(2,1)}, bf16[32,128,256]{2,1,0:T(8,128)(2,1)}, u32[]{:S(2)}, u32[]{:S(2)}) collective-permute-start(bf16[32,128,256]{2,1,0:T(8,128)(2,1)} %pad_maximum_fusion.2.refs_0_), channel_id=1, source_target_pairs={{0,4},{1,5},{2,6},{3,7},{4,8},{5,9},{6,10},{7,11},{8,12},{9,13},{1... | collective-permute-start | bytes 6291464 | tf_op jit(solution)/shard_map/ppermute | solution.py:178
  326.1 90.5 %collective-permute-start.61 = (bf16[1,32,32,256]{3,2,1,0:T(8,128)(2,1)S(1)}, bf16[1,32,32,256]{3,2,1,0:T(8,128)(2,1)S(1)}, u32[]{:S(2)}, u32[]{:S(2)}) collective-permute-start(bf16[1,32,32,256]{3,2,1,0:T(8,128)(2,1)S(1)} %slice.277), channel_id=1, source_target_pairs={{0,19},{1,18},{2,17},{3,16},{4,23},{5,22},{6,21},{7,20},{8,27},{9,... | collective-permute-start | bytes 1572872 | tf_op jit(solution)/shard_map/ppermute | solution.py:162
  326.1 92.0 %collective-permute-start.57 = (bf16[1,32,32,256]{3,2,1,0:T(8,128)(2,1)S(1)}, bf16[1,32,32,256]{3,2,1,0:T(8,128)(2,1)S(1)}, u32[]{:S(2)}, u32[]{:S(2)}) collective-permute-start(bf16[1,32,32,256]{3,2,1,0:T(8,128)(2,1)S(1)} %slice.273), channel_id=1, source_target_pairs={{0,18},{1,19},{2,16},{3,17},{4,22},{5,23},{6,20},{7,21},{8,26},{9,... | collective-permute-start | bytes 1572872 | tf_op jit(solution)/shard_map/ppermute | solution.py:162
  371.0 49.0 %collective-permute-start.53 = (bf16[1,32,32,256]{3,2,1,0:T(8,128)(2,1)S(1)}, bf16[1,32,32,256]{3,2,1,0:T(8,128)(2,1)S(1)}, u32[]{:S(2)}, u32[]{:S(2)}) collective-permute-start(bf16[1,32,32,256]{3,2,1,0:T(8,128)(2,1)S(1)} %slice.269), channel_id=1, source_target_pairs={{0,17},{1,16},{2,19},{3,18},{4,21},{5,20},{6,23},{7,22},{8,25},{9,... | collective-permute-start | bytes 1572872 | tf_op jit(solution)/shard_map/ppermute | solution.py:162
  371.1 108.9 %collective-permute-start.34 = (bf16[32,128,256]{2,1,0:T(8,128)(2,1)}, bf16[32,128,256]{2,1,0:T(8,128)(2,1)S(1)}, u32[]{:S(2)}, u32[]{:S(2)}) collective-permute-start(bf16[32,128,256]{2,1,0:T(8,128)(2,1)} %collective-permute-done.33.refs_4_), channel_id=1, source_target_pairs={{4,0},{5,1},{6,2},{7,3},{8,4},{9,5},{10,6},{11,7},{20,16},{21,17},... | collective-permute-start | bytes 6291464 | tf_op jit(solution)/shard_map/ppermute | solution.py:178
  415.0 65.7 %collective-permute-start.31 = (bf16[32,128,256]{2,1,0:T(8,128)(2,1)}, bf16[32,128,256]{2,1,0:T(8,128)(2,1)S(1)}, u32[]{:S(2)}, u32[]{:S(2)}) collective-permute-start(bf16[32,128,256]{2,1,0:T(8,128)(2,1)} %collective-permute-done.30.refs_1_), channel_id=1, source_target_pairs={{4,8},{5,9},{6,10},{7,11},{8,12},{9,13},{10,14},{11,15},{20,24},{2... | collective-permute-start | bytes 6291464 | tf_op jit(solution)/shard_map/ppermute | solution.py:178
  420.0 33.9 %collective-permute-start.56 = (bf16[1,32,32,256]{3,2,1,0:T(8,128)(2,1)S(1)}, bf16[1,32,32,256]{3,2,1,0:T(8,128)(2,1)S(1)}, u32[]{:S(2)}, u32[]{:S(2)}) collective-permute-start(bf16[1,32,32,256]{3,2,1,0:T(8,128)(2,1)S(1)} %slice.272), channel_id=1, source_target_pairs={{0,18},{1,19},{2,16},{3,17},{4,22},{5,23},{6,20},{7,21},{8,26},{9,... | collective-permute-start | bytes 1572872 | tf_op jit(solution)/shard_map/ppermute | solution.py:162
  431.5 32.7 %collective-permute-start.52 = (bf16[1,32,32,256]{3,2,1,0:T(8,128)(2,1)S(1)}, bf16[1,32,32,256]{3,2,1,0:T(8,128)(2,1)S(1)}, u32[]{:S(2)}, u32[]{:S(2)}) collective-permute-start(bf16[1,32,32,256]{3,2,1,0:T(8,128)(2,1)S(1)} %slice.268), channel_id=1, source_target_pairs={{0,17},{1,16},{2,19},{3,18},{4,21},{5,20},{6,23},{7,22},{8,25},{9,... | collective-permute-start | bytes 1572872 | tf_op jit(solution)/shard_map/ppermute | solution.py:162
  441.7 32.8 %collective-permute-start.48 = (bf16[1,32,32,256]{3,2,1,0:T(8,128)(2,1)S(1)}, bf16[1,32,32,256]{3,2,1,0:T(8,128)(2,1)S(1)}, u32[]{:S(2)}, u32[]{:S(2)}) collective-permute-start(bf16[1,32,32,256]{3,2,1,0:T(8,128)(2,1)S(1)} %slice.264), channel_id=1, source_target_pairs={{0,16},{1,17},{2,18},{3,19},{4,20},{5,21},{6,22},{7,23},{8,24},{9,... | collective-permute-start | bytes 1572872 | tf_op jit(solution)/shard_map/ppermute | solution.py:162
  464.2 40.3 %collective-permute-start.25 = (bf16[32,128,256]{2,1,0:T(8,128)(2,1)}, bf16[32,128,256]{2,1,0:T(8,128)(2,1)}, u32[]{:S(2)}, u32[]{:S(2)}) collective-permute-start(bf16[32,128,256]{2,1,0:T(8,128)(2,1)} %collective-permute-done.24.refs_4_), channel_id=1, source_target_pairs={{4,0},{5,1},{6,2},{7,3},{8,4},{9,5},{10,6},{11,7},{20,16},{21,17},... | collective-permute-start | bytes 6291464 | tf_op jit(solution)/shard_map/ppermute | solution.py:178
  474.6 51.1 %collective-permute-start.22 = (bf16[32,128,256]{2,1,0:T(8,128)(2,1)}, bf16[32,128,256]{2,1,0:T(8,128)(2,1)}, u32[]{:S(2)}, u32[]{:S(2)}) collective-permute-start(bf16[32,128,256]{2,1,0:T(8,128)(2,1)} %collective-permute-done.21.refs_1_), channel_id=1, source_target_pairs={{4,8},{5,9},{6,10},{7,11},{8,12},{9,13},{10,14},{11,15},{20,24},{2... | collective-permute-start | bytes 6291464 | tf_op jit(solution)/shard_map/ppermute | solution.py:178
  479.9 50.2 %collective-permute-start.35 = (bf16[32,128,256]{2,1,0:T(8,128)(2,1)S(1)}, bf16[32,128,256]{2,1,0:T(8,128)(2,1)S(1)}, u32[]{:S(2)}, u32[]{:S(2)}) collective-permute-start(bf16[32,128,256]{2,1,0:T(8,128)(2,1)S(1)} %collective-permute-done.34.refs_5_), channel_id=1, source_target_pairs={{4,0},{5,1},{6,2},{7,3},{20,16},{21,17},{22,18},{23,19}} | collective-permute-start | bytes 6291464 | tf_op jit(solution)/shard_map/ppermute | solution.py:178
  480.8 89.8 %collective-permute-start.32 = (bf16[32,128,256]{2,1,0:T(8,128)(2,1)S(1)}, bf16[32,128,256]{2,1,0:T(8,128)(2,1)S(1)}, u32[]{:S(2)}, u32[]{:S(2)}) collective-permute-start(bf16[32,128,256]{2,1,0:T(8,128)(2,1)S(1)} %collective-permute-done.31.refs_2_), channel_id=1, source_target_pairs={{8,12},{9,13},{10,14},{11,15},{24,28},{25,29},{26,30},{27,31}} | collective-permute-start | bytes 6291464 | tf_op jit(solution)/shard_map/ppermute | solution.py:178
  504.5 102.6 %collective-permute-start.26 = (bf16[32,128,256]{2,1,0:T(8,128)(2,1)}, bf16[32,128,256]{2,1,0:T(8,128)(2,1)}, u32[]{:S(2)}, u32[]{:S(2)}) collective-permute-start(bf16[32,128,256]{2,1,0:T(8,128)(2,1)} %collective-permute-done.25.refs_5_), channel_id=1, source_target_pairs={{4,0},{5,1},{6,2},{7,3},{20,16},{21,17},{22,18},{23,19}} | collective-permute-start | bytes 6291464 | tf_op jit(solution)/shard_map/ppermute | solution.py:178
  525.7 87.1 %collective-permute-start.23 = (bf16[32,128,256]{2,1,0:T(8,128)(2,1)}, bf16[32,128,256]{2,1,0:T(8,128)(2,1)}, u32[]{:S(2)}, u32[]{:S(2)}) collective-permute-start(bf16[32,128,256]{2,1,0:T(8,128)(2,1)} %collective-permute-done.22.refs_2_), channel_id=1, source_target_pairs={{8,12},{9,13},{10,14},{11,15},{24,28},{25,29},{26,30},{27,31}} | collective-permute-start | bytes 6291464 | tf_op jit(solution)/shard_map/ppermute | solution.py:178
  530.1 73.7 %collective-permute-start.44 = (bf16[2,32,32,256]{3,2,1,0:T(8,128)(2,1)}, bf16[2,32,32,256]{3,2,1,0:T(8,128)(2,1)S(1)}, u32[]{:S(2)}, u32[]{:S(2)}) collective-permute-start(bf16[2,32,32,256]{3,2,1,0:T(8,128)(2,1)} %slice.257), channel_id=1, source_target_pairs={{0,3},{1,2},{2,1},{3,0},{4,7},{5,6},{6,5},{7,4},{8,11},{9,10},{10,... | collective-permute-start | bytes 3145736 | tf_op jit(solution)/shard_map/ppermute | solution.py:151
  530.2 75.2 %collective-permute-start.40 = (bf16[2,32,32,256]{3,2,1,0:T(8,128)(2,1)}, bf16[2,32,32,256]{3,2,1,0:T(8,128)(2,1)S(1)}, u32[]{:S(2)}, u32[]{:S(2)}) collective-permute-start(bf16[2,32,32,256]{3,2,1,0:T(8,128)(2,1)} %slice.249), channel_id=1, source_target_pairs={{0,2},{1,3},{2,0},{3,1},{4,6},{5,7},{6,4},{7,5},{8,10},{9,11},{10,... | collective-permute-start | bytes 3145736 | tf_op jit(solution)/shard_map/ppermute | solution.py:151
  571.8 34.7 %collective-permute-start.36 = (bf16[2,32,32,256]{3,2,1,0:T(8,128)(2,1)}, bf16[2,32,32,256]{3,2,1,0:T(8,128)(2,1)S(1)}, u32[]{:S(2)}, u32[]{:S(2)}) collective-permute-start(bf16[2,32,32,256]{3,2,1,0:T(8,128)(2,1)} %slice.241), channel_id=1, source_target_pairs={{0,1},{1,0},{2,3},{3,2},{4,5},{5,4},{6,7},{7,6},{8,9},{9,8},{10,11... | collective-permute-start | bytes 3145736 | tf_op jit(solution)/shard_map/ppermute | solution.py:151
  603.9 39.9 %collective-permute-start.63 = (bf16[1,32,32,256]{3,2,1,0:T(8,128)(2,1)}, bf16[1,32,32,256]{3,2,1,0:T(8,128)(2,1)S(1)}, u32[]{:S(2)}, u32[]{:S(2)}) collective-permute-start(bf16[1,32,32,256]{3,2,1,0:T(8,128)(2,1)} %slice.279), channel_id=1, source_target_pairs={{0,19},{1,18},{2,17},{3,16},{4,23},{5,22},{6,21},{7,20},{8,27},{9,... | collective-permute-start | bytes 1572872 | tf_op jit(solution)/shard_map/ppermute | solution.py:162
  605.4 93.9 %collective-permute-start.47 = (bf16[2,32,32,256]{3,2,1,0:T(8,128)(2,1)S(1)}, bf16[2,32,32,256]{3,2,1,0:T(8,128)(2,1)S(1)}, u32[]{:S(2)}, u32[]{:S(2)}) collective-permute-start(bf16[2,32,32,256]{3,2,1,0:T(8,128)(2,1)S(1)} %slice.263), channel_id=1, source_target_pairs={{0,3},{1,2},{2,1},{3,0},{4,7},{5,6},{6,5},{7,4},{8,11},{9,10},{10,... | collective-permute-start | bytes 3145736 | tf_op jit(solution)/shard_map/ppermute | solution.py:151
  606.6 37.3 %collective-permute-start.59 = (bf16[1,32,32,256]{3,2,1,0:T(8,128)(2,1)}, bf16[1,32,32,256]{3,2,1,0:T(8,128)(2,1)S(1)}, u32[]{:S(2)}, u32[]{:S(2)}) collective-permute-start(bf16[1,32,32,256]{3,2,1,0:T(8,128)(2,1)} %slice.275), channel_id=1, source_target_pairs={{0,18},{1,19},{2,16},{3,17},{4,22},{5,23},{6,20},{7,21},{8,26},{9,... | collective-permute-start | bytes 1572872 | tf_op jit(solution)/shard_map/ppermute | solution.py:162
  607.0 37.4 %collective-permute-start.55 = (bf16[1,32,32,256]{3,2,1,0:T(8,128)(2,1)S(1)}, bf16[1,32,32,256]{3,2,1,0:T(8,128)(2,1)S(1)}, u32[]{:S(2)}, u32[]{:S(2)}) collective-permute-start(bf16[1,32,32,256]{3,2,1,0:T(8,128)(2,1)S(1)} %slice.271), channel_id=1, source_target_pairs={{0,17},{1,16},{2,19},{3,18},{4,21},{5,20},{6,23},{7,22},{8,25},{9,... | collective-permute-start | bytes 1572872 | tf_op jit(solution)/shard_map/ppermute | solution.py:162
  612.8 39.8 %collective-permute-start.51 = (bf16[1,32,32,256]{3,2,1,0:T(8,128)(2,1)S(1)}, bf16[1,32,32,256]{3,2,1,0:T(8,128)(2,1)S(1)}, u32[]{:S(2)}, u32[]{:S(2)}) collective-permute-start(bf16[1,32,32,256]{3,2,1,0:T(8,128)(2,1)S(1)} %slice.267), channel_id=1, source_target_pairs={{0,16},{1,17},{2,18},{3,19},{4,20},{5,21},{6,22},{7,23},{8,24},{9,... | collective-permute-start | bytes 1572872 | tf_op jit(solution)/shard_map/ppermute | solution.py:162
  643.9 32.2 %collective-permute-start.58 = (bf16[1,32,32,256]{3,2,1,0:T(8,128)(2,1)S(1)}, bf16[1,32,32,256]{3,2,1,0:T(8,128)(2,1)S(1)}, u32[]{:S(2)}, u32[]{:S(2)}) collective-permute-start(bf16[1,32,32,256]{3,2,1,0:T(8,128)(2,1)S(1)} %slice.274), channel_id=1, source_target_pairs={{0,18},{1,19},{2,16},{3,17},{4,22},{5,23},{6,20},{7,21},{8,26},{9,... | collective-permute-start | bytes 1572872 | tf_op jit(solution)/shard_map/ppermute | solution.py:162
  644.4 41.0 %collective-permute-start.54 = (bf16[1,32,32,256]{3,2,1,0:T(8,128)(2,1)S(1)}, bf16[1,32,32,256]{3,2,1,0:T(8,128)(2,1)S(1)}, u32[]{:S(2)}, u32[]{:S(2)}) collective-permute-start(bf16[1,32,32,256]{3,2,1,0:T(8,128)(2,1)S(1)} %slice.270), channel_id=1, source_target_pairs={{0,17},{1,16},{2,19},{3,18},{4,21},{5,20},{6,23},{7,22},{8,25},{9,... | collective-permute-start | bytes 1572872 | tf_op jit(solution)/shard_map/ppermute | solution.py:162
  652.6 44.4 %collective-permute-start.50 = (bf16[1,32,32,256]{3,2,1,0:T(8,128)(2,1)S(1)}, bf16[1,32,32,256]{3,2,1,0:T(8,128)(2,1)S(1)}, u32[]{:S(2)}, u32[]{:S(2)}) collective-permute-start(bf16[1,32,32,256]{3,2,1,0:T(8,128)(2,1)S(1)} %slice.266), channel_id=1, source_target_pairs={{0,16},{1,17},{2,18},{3,19},{4,20},{5,21},{6,22},{7,23},{8,24},{9,... | collective-permute-start | bytes 1572872 | tf_op jit(solution)/shard_map/ppermute | solution.py:162
  664.4 55.9 %collective-permute-start.43 = (bf16[2,32,32,256]{3,2,1,0:T(8,128)(2,1)}, bf16[2,32,32,256]{3,2,1,0:T(8,128)(2,1)}, u32[]{:S(2)}, u32[]{:S(2)}) collective-permute-start(bf16[2,32,32,256]{3,2,1,0:T(8,128)(2,1)} %slice.255), channel_id=1, source_target_pairs={{0,2},{1,3},{2,0},{3,1},{4,6},{5,7},{6,4},{7,5},{8,10},{9,11},{10,... | collective-permute-start | bytes 3145736 | tf_op jit(solution)/shard_map/ppermute | solution.py:151
  676.9 43.4 %collective-permute-start.39 = (bf16[2,32,32,256]{3,2,1,0:T(8,128)(2,1)}, bf16[2,32,32,256]{3,2,1,0:T(8,128)(2,1)}, u32[]{:S(2)}, u32[]{:S(2)}) collective-permute-start(bf16[2,32,32,256]{3,2,1,0:T(8,128)(2,1)} %slice.247), channel_id=1, source_target_pairs={{0,1},{1,0},{2,3},{3,2},{4,5},{5,4},{6,7},{7,6},{8,9},{9,8},{10,11... | collective-permute-start | bytes 3145736 | tf_op jit(solution)/shard_map/ppermute | solution.py:151
  686.2 34.3 %collective-permute-start.46 = (bf16[2,32,32,256]{3,2,1,0:T(8,128)(2,1)}, bf16[2,32,32,256]{3,2,1,0:T(8,128)(2,1)}, u32[]{:S(2)}, u32[]{:S(2)}) collective-permute-start(bf16[2,32,32,256]{3,2,1,0:T(8,128)(2,1)} %slice.261), channel_id=1, source_target_pairs={{0,3},{1,2},{2,1},{3,0},{4,7},{5,6},{6,5},{7,4},{8,11},{9,10},{10,... | collective-permute-start | bytes 3145736 | tf_op jit(solution)/shard_map/ppermute | solution.py:151
  697.8 45.2 %collective-permute-start.42 = (bf16[2,32,32,256]{3,2,1,0:T(8,128)(2,1)}, bf16[2,32,32,256]{3,2,1,0:T(8,128)(2,1)}, u32[]{:S(2)}, u32[]{:S(2)}) collective-permute-start(bf16[2,32,32,256]{3,2,1,0:T(8,128)(2,1)} %slice.253), channel_id=1, source_target_pairs={{0,2},{1,3},{2,0},{3,1},{4,6},{5,7},{6,4},{7,5},{8,10},{9,11},{10,... | collective-permute-start | bytes 3145736 | tf_op jit(solution)/shard_map/ppermute | solution.py:151
  700.3 42.6 %collective-permute-start.38 = (bf16[2,32,32,256]{3,2,1,0:T(8,128)(2,1)}, bf16[2,32,32,256]{3,2,1,0:T(8,128)(2,1)}, u32[]{:S(2)}, u32[]{:S(2)}) collective-permute-start(bf16[2,32,32,256]{3,2,1,0:T(8,128)(2,1)} %slice.245), channel_id=1, source_target_pairs={{0,1},{1,0},{2,3},{3,2},{4,5},{5,4},{6,7},{7,6},{8,9},{9,8},{10,11... | collective-permute-start | bytes 3145736 | tf_op jit(solution)/shard_map/ppermute | solution.py:151
  (77 other events, 1829.9 us)
